TPU v7x, 512 devices: a whole 4x8x8 slice. The times are simulated.
512 devices in a mesh: outer: 4 (over x), grp: 16 (over z, core), span: 8 (over y).
Axes of the slice: x: 4, y: 8, z: 8, core: 2. Of those that a mesh axis runs over, the one named last changes fastest.
Arguments:
- embeddings: bfloat16 [131072, 1024], P(('outer', 'grp', 'span')), parts along dimension 0, may hold values from -6 to 6
- cluster_id: int32 [131072], P(('outer', 'grp', 'span')), parts along dimension 0, may hold values from 0 to 15, as said below
- member_order: int32 [131072], P(('outer', 'grp', 'span')), parts along dimension 0, may hold values from 0 to 32767, each once
Outputs:
- best_earlier: float32 [131072], P(('outer', 'grp', 'span')), parts along dimension 0
There are 4 independent parts, one for each index of `outer`. A program takes and returns all parts, laid end to end along the dimension named above; each array names one. Nothing has to cross between parts.
Inputs may be any that keep to these rules, and one draw needn't show every extreme that they name: `cluster_id`: cluster c belongs to owner group c. The 256 embeddings of one device name clusters of one owner group at most 32 times; in every draw one owner group is named exactly 32 times by every device.
All inputs are finite; a program needn't handle non-finite values.
Results may differ from a plain program's by a relative error of at most 0.0003.
Values may be sent and summed in bfloat16 or wider, within the bound.
No kernel may reach another device: no remote copies, remote signals or barrier semaphores. Data moves between devices by JAX's collectives and lax.ppermute only.
A program may use at most 64 MiB of HBM per device.

v0:
```python
import jax
import jax.numpy as jnp
from jax import lax
from jax.sharding import PartitionSpec as P

CL_GRP = 1


def inverse_norms(block_rows):
    widened = block_rows.astype(jnp.float32)
    return lax.rsqrt(jnp.sum(widened * widened, axis=1) + 1e-06)


def cosines(left_rows, left_norm, right_rows, right_norm):
    products = lax.dot_general(
        left_rows, right_rows, (((1,), (1,)), ((), ())), preferred_element_type=jnp.float32
    )
    return products * left_norm[:, None] * right_norm[None, :]


def per_device(embeddings, cluster_id, member_order):
    row_count = embeddings.shape[0]
    group_count = lax.axis_size("grp")
    capacity = 2 * row_count // group_count
    slot_count = group_count * capacity
    owner_group = cluster_id // CL_GRP
    onehot = (owner_group[:, None] == jnp.arange(group_count, dtype=jnp.int32)[None, :]).astype(
        jnp.int32
    )
    position = jnp.sum((jnp.cumsum(onehot, axis=0) - onehot) * onehot, axis=1)
    slot_index = owner_group * capacity + position
    slot_source = (
        jnp.full((slot_count,), row_count, jnp.int32)
        .at[slot_index]
        .set(jnp.arange(row_count, dtype=jnp.int32))
    )
    padded_rows = jnp.concatenate(
        [embeddings, jnp.zeros((1, embeddings.shape[1]), embeddings.dtype)], axis=0
    )
    empty_mark = jnp.full((1,), -1, jnp.int32)
    send_rows = padded_rows[slot_source]
    send_cluster = jnp.concatenate([cluster_id, empty_mark])[slot_source]
    send_order = jnp.concatenate([member_order, empty_mark])[slot_source]
    own_rows, own_cluster, own_order = (
        lax.all_to_all(send_rows, "grp", split_axis=0, concat_axis=0, tiled=True),
        lax.all_to_all(send_cluster, "grp", split_axis=0, concat_axis=0, tiled=True),
        lax.all_to_all(send_order, "grp", split_axis=0, concat_axis=0, tiled=True),
    )
    own_norm = inverse_norms(own_rows)
    initial = jnp.full((slot_count,), -1.0, jnp.float32)
    other_rows = lax.all_gather(own_rows, "span", axis=0, tiled=True)
    other_cluster = lax.all_gather(own_cluster, "span", axis=0, tiled=True)
    other_order = lax.all_gather(own_order, "span", axis=0, tiled=True)
    scores = cosines(own_rows, own_norm, other_rows, inverse_norms(other_rows))
    earlier = (
        (own_cluster[:, None] == other_cluster[None, :])
        & (other_cluster[None, :] >= 0)
        & (other_order[None, :] < own_order[:, None])
    )
    best_cosine = jnp.maximum(
        initial, jnp.max(jnp.where(earlier, scores, jnp.float32(-1.0)), axis=1)
    )
    home_maxima = lax.all_to_all(best_cosine, "grp", split_axis=0, concat_axis=0, tiled=True)
    return home_maxima[slot_index]


def solution(mesh):
    return jax.shard_map(
        per_device,
        mesh=mesh,
        in_specs=(
            P(("outer", "grp", "span"), None),
            P(("outer", "grp", "span")),
            P(("outer", "grp", "span")),
        ),
        out_specs=P(("outer", "grp", "span")),
        check_vma=False,
    )
```

profile of v0, /device:TPU:1, one launch (start us, length us, event | category | flops | bytes accessed | tf_op | source)
XLA Modules:
  0.0 187.3 jit_solution(7654427032840841903)
XLA Ops:
  6.5 0.8 fusion.3
  7.3 0.6 reduce-window.6
  8.1 0.8 fusion.2
  8.9 0.7 compare_select_fusion.1
  9.6 1.4 scatter_custom_fusion
  11.0 1.1 concatenate.11
  12.1 2.1 %gather_fusion.2 = bf16[512,1024]{1,0:T(8,128)(2,1)S(1)} fusion(bf16[257,1024]{1,0:T(8,128)(2,1)S(1)} %concatenate.11, s32[1024]{0:T(1024)S(1)} %pad_clamp_fusion.1), kind=kCustom, calls=%fused_computation.2 | custom fusion | bytes 2099200 | tf_op jit(solution)/shard_map/gather | solution.py:41
  14.1 40.3 %all_to_all.42 = bf16[16,32,1024]{2,1,0:T(8,128)(2,1)} all-to-all(bf16[16,32,1024]{2,1,0:T(8,128)(2,1)S(1)} %bitcast.37), channel_id=1, replica_groups=mesh['outer'=4,'grp'=16,'span'=8] {'grp'}, dimensions={0} | all-to-all | bytes 2097152 | tf_op jit(solution)/shard_map/all_to_all | solution.py:45
  54.5 3.5 %gather_fusion.1 = s32[512]{0:T(512)S(1)} fusion(s32[257]{0:T(512)S(1)} %get-tuple-element.5, s32[1024]{0:T(1024)S(1)} %pad_clamp_fusion.1), kind=kCustom, calls=%fused_computation.1 | custom fusion | bytes 6144 | tf_op jit(solution)/shard_map/gather | solution.py:43
  58.0 0.7 all_to_all.30
  58.6 3.4 %all-to-all-start.1 = ((s32[16,32,1]{1,2,0:T(1,128)}), s32[16,32,1]{1,2,0:T(1,128)S(1)}, u32[]{:S(2)}, u32[]{:S(2)}) async-start(s32[16,32,1]{1,2,0:T(1,128)} %bitcast.4), calls=%async_computation.1 | async-start | bytes 16384 | tf_op jit(solution)/shard_map/all_to_all | solution.py:47
  62.0 3.5 %gather_fusion = s32[512]{0:T(512)S(1)} fusion(s32[257]{0:T(512)S(1)} %get-tuple-element.6, s32[1024]{0:T(1024)S(1)} %pad_clamp_fusion.1), kind=kCustom, calls=%fused_computation | custom fusion | bytes 6144 | tf_op jit(solution)/shard_map/gather | solution.py:42
  65.5 0.7 all_to_all.28
  66.2 2.4 %all-to-all-done.1 = s32[16,32,1]{1,2,0:T(1,128)S(1)} async-done(((s32[16,32,1]{1,2,0:T(1,128)}), s32[16,32,1]{1,2,0:T(1,128)S(1)}, u32[]{:S(2)}, u32[]{:S(2)}) %all-to-all-start.1) | async-done | bytes 2080 | tf_op jit(solution)/shard_map/all_to_all | solution.py:47
  68.6 4.4 %all-to-all-start = ((s32[16,32,1]{1,2,0:T(1,128)}), s32[16,32,1]{1,2,0:T(1,128)S(1)}, u32[]{:S(2)}, u32[]{:S(2)}) async-start(s32[16,32,1]{1,2,0:T(1,128)} %bitcast.2), calls=%async_computation | async-start | bytes 16384 | tf_op jit(solution)/shard_map/all_to_all | solution.py:46
  73.0 0.5 broadcast.92
  73.5 0.7 reduce.16
  74.3 5.7 %all-to-all-done = s32[16,32,1]{1,2,0:T(1,128)S(1)} async-done(((s32[16,32,1]{1,2,0:T(1,128)}), s32[16,32,1]{1,2,0:T(1,128)S(1)}, u32[]{:S(2)}, u32[]{:S(2)}) %all-to-all-start) | async-done | bytes 2080 | tf_op jit(solution)/shard_map/all_to_all | solution.py:46
  80.1 0.7 reduce.17
  80.8 20.8 %all-gather = s32[8,1,512]{2,1,0:T(1,128)S(1)} all-gather(s32[1,1,512]{2,1,0:T(1,128)S(1)} %reshape.105), channel_id=1, replica_groups=mesh['outer'=4,'grp'=16,'span'=8] {'span'}, dimensions={0}, use_global_device_ids=true | all-gather | bytes 18432 | tf_op jit(solution)/shard_map/all_gather | solution.py:52
  101.6 18.0 %all-gather.1 = s32[8,1,512]{2,1,0:T(1,128)S(1)} all-gather(s32[1,1,512]{2,1,0:T(1,128)S(1)} %reshape.107), channel_id=1, replica_groups=mesh['outer'=4,'grp'=16,'span'=8] {'span'}, dimensions={0}, use_global_device_ids=true | all-gather | bytes 18432 | tf_op jit(solution)/shard_map/all_gather | solution.py:53
  119.7 1.5 multiply_reduce_fusion.1
  121.3 27.0 %all-gather.4.cloned.1.call-done = bf16[4096,1024]{1,0:T(8,128)(2,1)} async-done(((bf16[512,1024]{1,0:T(8,128)(2,1)}), bf16[4096,1024]{1,0:T(8,128)(2,1)}) %all-gather.4.cloned.1.call-update) | async-done | bytes 8388624 | tf_op jit(solution)/shard_map/all_gather | solution.py:51
  148.2 5.2 %multiply_reduce_fusion = f32[4096]{0:T(1024)S(1)} fusion(bf16[4096,1024]{1,0:T(8,128)(2,1)} %all-gather.4.cloned.1.call-done), kind=kLoop, calls=%fused_computation.5 | loop fusion | flops 12578816 | bytes 8404992 | tf_op jit(solution)/shard_map/reduce_sum | solution.py:11
  153.5 0.5 copy-done.1
  154.0 6.9 %select_reduce_fusion = f32[512]{0:T(512)S(1)} fusion(bf16[512,1024]{1,0:T(8,128)(2,1)S(1)} %bitcast.36, bf16[4096,1024]{1,0:T(8,128)(2,1)S(1)} %copy-done.1, f32[4096]{0:T(1024)S(1)} %add_rsqrt_fusion, f32[512]{0:T(512)S(1)} %rsqrt.18, s32[4096]{0:T(1024)S(1)} %bitcast.43, s32[4096]{0:T(1024)S(1)} %bitcast.41, s32[512]{0:T(512)S(1)} %all_to_all.32, ...), kind=kOutput, calls=%fused_computation.6 | convolution fusion | flops 4311744000 | bytes 9498624 | tf_op jit(solution)/shard_map/dot_general | solution.py:15
  160.9 0.7 max_broadcast_in_dim.14
  161.6 8.1 %all-to-all-start.3 = ((f32[16,32,1]{1,2,0:T(1,128)}), f32[16,32,1]{1,2,0:T(1,128)S(1)}, u32[]{:S(2)}, u32[]{:S(2)}) async-start(f32[16,32,1]{1,2,0:T(1,128)} %bitcast.8), calls=%async_computation.3 | async-start | bytes 16384 | tf_op jit(solution)/shard_map/all_to_all | solution.py:63
  169.7 7.0 %all-to-all-done.3 = f32[16,32,1]{1,2,0:T(1,128)S(1)} async-done(((f32[16,32,1]{1,2,0:T(1,128)}), f32[16,32,1]{1,2,0:T(1,128)S(1)}, u32[]{:S(2)}, u32[]{:S(2)}) %all-to-all-start.3) | async-done | bytes 2080 | tf_op jit(solution)/shard_map/all_to_all | solution.py:63
  176.7 0.5 broadcast.94
  177.2 0.7 reduce.18
  178.0 2.5 %gather_fusion.3 = f32[256]{0:T(256)} fusion(f32[512]{0:T(512)S(1)} %all_to_all.37, s32[1024]{0:T(1024)S(1)} %pad_clamp_fusion), kind=kCustom, calls=%fused_computation.3 | custom fusion | bytes 3072 | tf_op jit(solution)/shard_map/gather | solution.py:64
  (27 shorter events, 0.8 us)
Async XLA Ops:
  6.5 47.9 %copy-start.2 = (s32[256]{0:T(256)S(1)}, s32[256]{0:T(256)}, u32[]{:S(2)}) copy-start(s32[256]{0:T(256)} %param.4) | copy-start | bytes 3076
  6.5 47.9 %copy-start.3 = (s32[256]{0:T(256)S(1)}, s32[256]{0:T(256)}, u32[]{:S(2)}) copy-start(s32[256]{0:T(256)} %param.5) | copy-start | bytes 3076
  6.5 141.7 %all-gather.4.cloned.1.call-start = ((), (), s32[]{:S(2)}) async-start(), calls=%async_computation.4 | async-start | bytes 9437184 | tf_op jit(solution)/shard_map/all_gather | solution.py:51
  54.4 99.1 %copy-start = (bf16[16,32,1024]{2,1,0:T(8,128)(2,1)S(1)}, bf16[16,32,1024]{2,1,0:T(8,128)(2,1)}, u32[]{:S(2)}) copy-start(bf16[16,32,1024]{2,1,0:T(8,128)(2,1)} %all_to_all.42) | copy-start | bytes 3145732
  58.6 9.9 %all-to-all-start.1 = ((s32[16,32,1]{1,2,0:T(1,128)}), s32[16,32,1]{1,2,0:T(1,128)S(1)}, u32[]{:S(2)}, u32[]{:S(2)}) async-start(s32[16,32,1]{1,2,0:T(1,128)} %bitcast.4), calls=%async_computation.1 | async-start | bytes 16384 | tf_op jit(solution)/shard_map/all_to_all | solution.py:47
  68.6 11.4 %all-to-all-start = ((s32[16,32,1]{1,2,0:T(1,128)}), s32[16,32,1]{1,2,0:T(1,128)S(1)}, u32[]{:S(2)}, u32[]{:S(2)}) async-start(s32[16,32,1]{1,2,0:T(1,128)} %bitcast.2), calls=%async_computation | async-start | bytes 16384 | tf_op jit(solution)/shard_map/all_to_all | solution.py:46
  148.2 5.8 %copy-start.1 = (bf16[4096,1024]{1,0:T(8,128)(2,1)S(1)}, bf16[4096,1024]{1,0:T(8,128)(2,1)}, u32[]{:S(2)}) copy-start(bf16[4096,1024]{1,0:T(8,128)(2,1)} %all-gather.4.cloned.1.call-done) | copy-start | bytes 25165828
  161.6 15.1 %all-to-all-start.3 = ((f32[16,32,1]{1,2,0:T(1,128)}), f32[16,32,1]{1,2,0:T(1,128)S(1)}, u32[]{:S(2)}, u32[]{:S(2)}) async-start(f32[16,32,1]{1,2,0:T(1,128)} %bitcast.8), calls=%async_computation.3 | async-start | bytes 16384 | tf_op jit(solution)/shard_map/all_to_all | solution.py:63
Sparse Core Ops, SparseCore 0:
  54.6 93.6 all-gather.3
where the time goes:
time: 188 us; the launch traced here: 187 us
  blocking collectives  79.1 us (42%)
  waiting for transfers between devices  42 us (22%)
  local copies, waits for them, and re-layouts  18.2 us (10%)
  starting transfers between devices  15.8 us (8%)
  between operations  13.5 us (7%)
  other arithmetic  11.6 us (6%)
  matrix products  6.94 us (4%)
    all_to_all x1, blocking collectives, per_device(): lax.all_to_all(send_rows, 'grp', split_axis=0, concat_axis=0, tiled=True)  40.3 us
    all_gather x1, waiting for transfers between devices, per_device(): other_rows = lax.all_gather(own_rows, 'span', axis=0, tiled=True)  27 us
    all_gather x1, blocking collectives, per_device(): other_cluster = lax.all_gather(own_cluster, 'span', axis=0, tiled=True)  20.8 us
    all_gather x1, blocking collectives, per_device(): other_order = lax.all_gather(own_order, 'span', axis=0, tiled=True)  18 us
    all_to_all x1, starting transfers between devices, per_device(): lax.all_to_all(best_cosine, 'grp', split_axis=0, concat_axis=0, tiled=True)  8.06 us
    all_to_all x1, waiting for transfers between devices, per_device(): lax.all_to_all(best_cosine, 'grp', split_axis=0, concat_axis=0, tiled=True)  7.02 us
    dot_general x1, matrix products, cosines(): lax.dot_general(left_rows, right_rows, (((1,), (1,)), ((), ())), preferre...  6.94 us
    reduce_sum x2, other arithmetic, inverse_norms(): return lax.rsqrt(jnp.sum(widened * widened, axis=1) + 1e-06)  6.74 us
  transfers between devices with their start and end apart: 4, of which 4 were waited for; matrix products, arithmetic and copies ran while one was open for 6% of the time, Pallas kernels for 0%

commit v1 on v0

v1 whole, which is shorter than its diff:
```python
import functools

import jax
import jax.numpy as jnp
from jax import lax
from jax.experimental import pallas as pl
from jax.experimental.pallas import tpu as pltpu
from jax.sharding import PartitionSpec as P

ROWS = 256
META = 16
AUG = ROWS + META
SPAN_ORDER = 32768
LOW = -1e30
VMEM_LIMIT = 48 * 1024 * 1024


def prepare_kernel(x_ref, cluster_ref, order_ref, aug_ref, norm_ref):
    rows = x_ref[...]
    wide = rows.astype(jnp.float32)
    column = lax.rsqrt(jnp.sum(wide * wide, axis=1, keepdims=True) + 1e-06)
    norm = jnp.broadcast_to(column, (ROWS, 128)).T[0:1, :]
    cluster = cluster_ref[...].astype(jnp.float32)
    order = order_ref[...]
    high = jnp.right_shift(order, 8).astype(jnp.float32)
    low = jnp.bitwise_and(order, 255).astype(jnp.float32)
    first = norm.astype(jnp.bfloat16).astype(jnp.float32)
    rest = norm - first
    second = rest.astype(jnp.bfloat16).astype(jnp.float32)
    third = rest - second
    line = lax.broadcasted_iota(jnp.int32, (META, ROWS), 0)
    meta = jnp.zeros((META, ROWS), jnp.float32)
    for index, values in enumerate((cluster, high, low, first, second, third)):
        meta = jnp.where(line == index, values, meta)
    aug_ref[0:ROWS, :] = rows
    aug_ref[ROWS:AUG, :] = jnp.zeros((META, rows.shape[1]), jnp.bfloat16)
    aug_ref[ROWS:AUG, 0:ROWS] = meta.astype(jnp.bfloat16)
    norm_ref[...] = norm


def prepare(x, cluster, order):
    return pl.pallas_call(
        prepare_kernel,
        out_shape=(
            jax.ShapeDtypeStruct((AUG, x.shape[1]), jnp.bfloat16),
            jax.ShapeDtypeStruct((1, ROWS), jnp.float32),
        ),
        compiler_params=pltpu.CompilerParams(vmem_limit_bytes=VMEM_LIMIT),
    )(x, cluster.reshape(1, ROWS), order.reshape(1, ROWS))


def read_meta(ref):
    meta = ref[ROWS:AUG, 0:ROWS].astype(jnp.float32)
    floor = meta[0:1] * float(SPAN_ORDER)
    key = floor + (meta[1:2] * 256.0 + meta[2:3])
    norm = meta[3:4] + (meta[4:5] + meta[5:6])
    return floor, key, norm


def fold_kernel(n_old_rows, n_new_rows, n_old_cols, n_new_cols, has_acc, *refs):
    refs = list(refs)
    take = lambda n: [refs.pop(0) for _ in range(n)]
    rows = take(n_old_rows + n_new_rows)
    cols = take(n_old_cols + n_new_cols)
    old_wide = take(n_old_cols)
    acc_in = take(1) if has_acc else []
    acc_ref = refs.pop(0)
    new_wide = take(n_new_cols)
    row_data, row_key, row_floor = refs
    n_rows = n_old_rows + n_new_rows

    for i, ref in enumerate(rows):
        row_data[i] = ref[0:ROWS, :]
        floor, key, _ = read_meta(ref)
        row_key[i] = jnp.broadcast_to(key, (8, ROWS))
        row_floor[i] = jnp.broadcast_to(floor, (8, ROWS))
    for ref, wide in zip(cols[n_old_cols:], new_wide):
        _, key, norm = read_meta(ref)
        for half in range(2):
            part = slice(half * 128, (half + 1) * 128)
            wide[part, 0:128] = jnp.broadcast_to(key[:, part], (128, 128)).T
            wide[part, 128:256] = jnp.broadcast_to(norm[:, part], (128, 128)).T
    wides = old_wide + new_wide

    def block(i, picked, best):
        right = row_data[i]
        for j in picked:
            score = lax.dot_general(
                cols[j][0:ROWS, :], right, (((1,), (1,)), ((), ())), preferred_element_type=jnp.float32
            )
            halves = []
            for half in range(2):
                part = slice(half * 128, (half + 1) * 128)
                key = wides[j][:, 0:128].reshape(ROWS // 8, 8, 128)
                norm = wides[j][:, 128:256].reshape(ROWS // 8, 8, 128)
                valid = (key < row_key[i, :, part]) & (key >= row_floor[i, :, part])
                scaled = score[:, part].reshape(ROWS // 8, 8, 128) * norm
                halves.append(jnp.max(jnp.where(valid, scaled, LOW), axis=0))
            best = jnp.maximum(best, jnp.concatenate(halves, axis=1))
        return best

    def old_row(i, carry):
        acc_ref[i] = block(i, range(n_old_cols, n_old_cols + n_new_cols), acc_in[0][i])
        return carry

    def new_row(i, carry):
        start = jnp.full((8, ROWS), LOW, jnp.float32)
        acc_ref[i] = block(i, range(n_old_cols + n_new_cols), start)
        return carry

    if n_old_rows and n_new_cols:
        lax.fori_loop(0, n_old_rows, old_row, 0)
    elif n_old_rows:
        acc_ref[0:n_old_rows] = acc_in[0][...]
    if n_new_rows:
        lax.fori_loop(n_old_rows, n_rows, new_row, 0)


def fold(old_rows, new_rows, old_cols, new_cols, old_wide, acc):
    n_rows = len(old_rows) + len(new_rows)
    has_acc = acc is not None
    width = (old_rows + new_rows)[0].shape[1]
    pairs = len(new_rows) * (len(old_cols) + len(new_cols)) + len(old_rows) * len(new_cols)
    args = [*old_rows, *new_rows, *old_cols, *new_cols, *old_wide, *([acc] if has_acc else [])]
    out = pl.pallas_call(
        functools.partial(
            fold_kernel, len(old_rows), len(new_rows), len(old_cols), len(new_cols), has_acc
        ),
        out_shape=(
            jax.ShapeDtypeStruct((n_rows, 8, ROWS), jnp.float32),
            *[jax.ShapeDtypeStruct((ROWS, 256), jnp.float32) for _ in new_cols],
        ),
        scratch_shapes=[
            pltpu.VMEM((n_rows, ROWS, width), jnp.bfloat16),
            pltpu.VMEM((n_rows, 8, ROWS), jnp.float32),
            pltpu.VMEM((n_rows, 8, ROWS), jnp.float32),
        ],
        compiler_params=pltpu.CompilerParams(vmem_limit_bytes=VMEM_LIMIT),
        cost_estimate=pl.CostEstimate(
            flops=2 * pairs * ROWS * ROWS * width, bytes_accessed=len(args) * AUG * width * 2, transcendentals=0
        ),
    )(*args)
    return out[0], list(out[1:])


def route_kernel(offsets, place_ref, acc_ref, out_ref):
    here = place_ref[0]
    for index, offset in enumerate(offsets):
        target = lax.rem(here + offset, 8)
        out_ref[pl.ds(target, 1), :] = jnp.max(acc_ref[index], axis=0, keepdims=True)


def route(acc, place, offsets):
    return pl.pallas_call(
        functools.partial(route_kernel, offsets),
        out_shape=jax.ShapeDtypeStruct((8, ROWS), jnp.float32),
        in_specs=[pl.BlockSpec(memory_space=pltpu.SMEM), pl.BlockSpec(memory_space=pltpu.VMEM)],
        out_specs=pl.BlockSpec(memory_space=pltpu.VMEM),
    )(place, acc)


def ring(axis, size, step):
    return [(i, (i + step) % size) for i in range(size)]


def per_device(embeddings, cluster_id, member_order):
    own, norm = prepare(embeddings, cluster_id, member_order)
    swap = lambda v: lax.ppermute(v, "grp", [(i, i ^ 1) for i in range(16)])
    y_up = lambda v: lax.ppermute(v, "span", ring("span", 8, 1))
    y_down = lambda v: lax.ppermute(v, "span", ring("span", 8, -1))
    z_up = lambda v: lax.ppermute(v, "grp", ring("grp", 16, 2))
    z_down = lambda v: lax.ppermute(v, "grp", ring("grp", 16, -2))

    ya, yb, za, zb = [own], [own], [own], [own]
    for _ in range(3):
        ya.append(y_up(ya[-1]))
        yb.append(y_down(yb[-1]))
        za.append(z_up(za[-1]))
        zb.append(z_down(zb[-1]))
    ya.append(y_up(ya[-1]))
    zb.append(z_down(zb[-1]))

    sibling = swap(own)

    def swapped(blocks):
        joined = swap(jnp.concatenate(blocks, axis=0))
        return [joined[AUG * i : AUG * (i + 1)] for i in range(len(blocks))]

    near = swapped([ya[1], yb[1], ya[2], yb[2]])
    far = swapped([ya[3], yb[3], ya[4]])

    rows, cols, wides, acc = [], [], [], None
    steps = [
        ([own, za[1], zb[1]], [own, sibling, ya[1], yb[1]]),
        ([za[2], zb[2]], [ya[2], yb[2]]),
        ([], near),
        ([za[3], zb[3]], [ya[3], yb[3]]),
        ([zb[4]], [ya[4]]),
        ([], far),
    ]
    for new_rows, new_cols in steps:
        acc, more = fold(rows, new_rows, cols, new_cols, wides if new_rows else [], acc) if new_rows else fold(
            rows, [], [], new_cols, [], acc
        )
        rows, cols, wides = rows + new_rows, cols + new_cols, wides + more

    offsets = (0, 7, 1, 6, 2, 5, 3, 4)
    place = (lax.axis_index("grp") // 2).astype(jnp.int32).reshape(1)
    outgoing = route(acc, place, offsets)
    groups = [[2 * z + core for z in range(8)] for core in range(2)]
    arrived = lax.all_to_all(
        outgoing, "grp", split_axis=0, concat_axis=0, tiled=True, axis_index_groups=groups
    )
    return jnp.maximum(jnp.max(arrived, axis=0) * norm[0], -1.0)


def solution(mesh):
    return jax.shard_map(
        per_device,
        mesh=mesh,
        in_specs=(
            P(("outer", "grp", "span"), None),
            P(("outer", "grp", "span")),
            P(("outer", "grp", "span")),
        ),
        out_specs=P(("outer", "grp", "span")),
        check_vma=False,
    )
```

time: 188 us -> 170 us (0.904)
  the two profiles are of different devices: /device:TPU:1 before, /device:TPU:2 now
where the time goes in v1:
time: 170 us; the launch traced here: 169 us
  starting transfers between devices  59.3 us (35%)
  Pallas kernels  44.5 us (26%)
  waiting for transfers between devices  41.6 us (24%)
  blocking collectives  10.1 us (6%)
  local copies, waits for them, and re-layouts  9.88 us (6%)
  other arithmetic  3.51 us (2%)
    pallas_call x6, Pallas kernels, fold(): pl.pallas_call(functools.partial(fold_kernel, len(old_rows), len(new_rows...  42.8 us
    ppermute x4, starting transfers between devices, per_device(): z_down = lambda v: lax.ppermute(v, 'grp', ring('grp', 16, -2))  25.3 us
    ppermute x3, waiting for transfers between devices, per_device(): y_down = lambda v: lax.ppermute(v, 'span', ring('span', 8, -1))  21.2 us
    ppermute x3, starting transfers between devices, per_device(): y_down = lambda v: lax.ppermute(v, 'span', ring('span', 8, -1))  12.9 us
    ppermute x4, waiting for transfers between devices, per_device(): z_down = lambda v: lax.ppermute(v, 'grp', ring('grp', 16, -2))  12.6 us
    all_to_all x1, blocking collectives, per_device(): lax.all_to_all(outgoing, 'grp', split_axis=0, concat_axis=0, tiled=True,...  10.1 us
    ppermute x4, starting transfers between devices, per_device(): y_up = lambda v: lax.ppermute(v, 'span', ring('span', 8, 1))  9.68 us
    ppermute x3, starting transfers between devices, per_device(): swap = lambda v: lax.ppermute(v, 'grp', [(i, i ^ 1) for i in range(16)])  5.74 us
  transfers between devices with their start and end apart: 17, of which 7 were waited for; matrix products, arithmetic and copies ran while one was open for 2% of the time, Pallas kernels for 21%

profile of v1, /device:TPU:2, one launch (start us, length us, event | category | flops | bytes accessed | tf_op | source)
XLA Modules:
  0.0 169.3 jit_solution(17655261314476869847)
XLA Ops:
  2.6 5.4 %collective-permute-start.10 = (bf16[272,1024]{1,0:T(8,128)(2,1)S(1)}, bf16[272,1024]{1,0:T(8,128)(2,1)S(1)}, u32[]{:S(2)}, u32[]{:S(2)}) collective-permute-start(bf16[272,1024]{1,0:T(8,128)(2,1)S(1)} %get-tuple-element.25.refs_0_.refs_3_.refs_5_.refs_7_.refs_8_), channel_id=1, source_target_pairs={{0,7},{1,0},{2,1},{3,2},{4,3},{5,4},{6,5},{7,6},{8,15},{9,8},{10,9... | collective-permute-start | bytes 1671176 | tf_op jit(solution)/shard_map/ppermute | solution.py:170
  8.0 1.9 %collective-permute-start.7 = (bf16[272,1024]{1,0:T(8,128)(2,1)S(1)}, bf16[272,1024]{1,0:T(8,128)(2,1)S(1)}, u32[]{:S(2)}, u32[]{:S(2)}) collective-permute-start(bf16[272,1024]{1,0:T(8,128)(2,1)S(1)} %get-tuple-element.25.refs_0_.refs_3_.refs_5_.refs_7_.refs_8_), channel_id=1, source_target_pairs={{0,1},{1,2},{2,3},{3,4},{4,5},{5,6},{6,7},{7,0},{8,9},{9,10},{10,1... | collective-permute-start | bytes 1671176 | tf_op jit(solution)/shard_map/ppermute | solution.py:169
  10.0 9.9 %collective-permute-done.10.refs_6_.refs_8_.refs_10_.refs_11_ = bf16[272,1024]{1,0:T(8,128)(2,1)S(1)} collective-permute-done((bf16[272,1024]{1,0:T(8,128)(2,1)S(1)}, bf16[272,1024]{1,0:T(8,128)(2,1)S(1)}, u32[]{:S(2)}, u32[]{:S(2)}) %collective-permute-start.10) | collective-permute-done | bytes 557088 | tf_op jit(solution)/shard_map/ppermute | solution.py:170
  19.9 5.6 %collective-permute-start.11 = (bf16[272,1024]{1,0:T(8,128)(2,1)S(1)}, bf16[272,1024]{1,0:T(8,128)(2,1)S(1)}, u32[]{:S(2)}, u32[]{:S(2)}) collective-permute-start(bf16[272,1024]{1,0:T(8,128)(2,1)S(1)} %collective-permute-done.10.refs_6_.refs_8_.refs_10_.refs_11_), channel_id=1, source_target_pairs={{0,7},{1,0},{2,1},{3,2},{4,3},{5,4},{6,5},{7,6},{8,15},{9,8},{10,9... | collective-permute-start | bytes 1671176 | tf_op jit(solution)/shard_map/ppermute | solution.py:170
  25.5 1.9 %collective-permute-start.8 = (bf16[272,1024]{1,0:T(8,128)(2,1)S(1)}, bf16[272,1024]{1,0:T(8,128)(2,1)S(1)}, u32[]{:S(2)}, u32[]{:S(2)}) collective-permute-start(bf16[272,1024]{1,0:T(8,128)(2,1)S(1)} %collective-permute-done.7.refs_5_.refs_7_.refs_9_.refs_10_), channel_id=1, source_target_pairs={{0,1},{1,2},{2,3},{3,4},{4,5},{5,6},{6,7},{7,0},{8,9},{9,10},{10,1... | collective-permute-start | bytes 1671176 | tf_op jit(solution)/shard_map/ppermute | solution.py:169
  27.4 9.0 %collective-permute-done.11.refs_10_.refs_12_.refs_13_ = bf16[272,1024]{1,0:T(8,128)(2,1)S(1)} collective-permute-done((bf16[272,1024]{1,0:T(8,128)(2,1)S(1)}, bf16[272,1024]{1,0:T(8,128)(2,1)S(1)}, u32[]{:S(2)}, u32[]{:S(2)}) %collective-permute-start.11) | collective-permute-done | bytes 557088 | tf_op jit(solution)/shard_map/ppermute | solution.py:170
  36.5 5.3 %collective-permute-done.8.refs_9_.refs_11_.refs_12_ = bf16[272,1024]{1,0:T(8,128)(2,1)S(1)} collective-permute-done((bf16[272,1024]{1,0:T(8,128)(2,1)S(1)}, bf16[272,1024]{1,0:T(8,128)(2,1)S(1)}, u32[]{:S(2)}, u32[]{:S(2)}) %collective-permute-start.8) | collective-permute-done | bytes 557088 | tf_op jit(solution)/shard_map/ppermute | solution.py:169
  43.4 1.9 %collective-permute-start.16 = (bf16[1088,1024]{1,0:T(8,128)(2,1)}, bf16[1088,1024]{1,0:T(8,128)(2,1)}, u32[]{:S(2)}, u32[]{:S(2)}) collective-permute-start(bf16[1088,1024]{1,0:T(8,128)(2,1)} %pad_maximum_fusion), channel_id=1, source_target_pairs={{0,8},{8,0},{16,24},{24,16},{32,40},{40,32},{48,56},{56,48},{64,72... | collective-permute-start | bytes 6684680 | tf_op jit(solution)/shard_map/ppermute | solution.py:168
  45.3 10.9 %collective-permute-start.1 = (bf16[272,1024]{1,0:T(8,128)(2,1)S(1)}, bf16[272,1024]{1,0:T(8,128)(2,1)S(1)}, u32[]{:S(2)}, u32[]{:S(2)}) collective-permute-start(bf16[272,1024]{1,0:T(8,128)(2,1)S(1)} %get-tuple-element.25.refs_0_.refs_3_.refs_5_.refs_7_.refs_8_), channel_id=1, source_target_pairs={{0,112},{8,120},{16,0},{24,8},{32,16},{40,24},{48,32},{56,40},{64,... | collective-permute-start | bytes 1671176 | tf_op jit(solution)/shard_map/ppermute | solution.py:172
  56.3 1.9 %collective-permute-start.9 = (bf16[272,1024]{1,0:T(8,128)(2,1)S(1)}, bf16[272,1024]{1,0:T(8,128)(2,1)S(1)}, u32[]{:S(2)}, u32[]{:S(2)}) collective-permute-start(bf16[272,1024]{1,0:T(8,128)(2,1)S(1)} %collective-permute-done.8.refs_9_.refs_11_.refs_12_), channel_id=1, source_target_pairs={{0,1},{1,2},{2,3},{3,4},{4,5},{5,6},{6,7},{7,0},{8,9},{9,10},{10,1... | collective-permute-start | bytes 1671176 | tf_op jit(solution)/shard_map/ppermute | solution.py:169
  58.2 1.9 %collective-permute-start = (bf16[272,1024]{1,0:T(8,128)(2,1)S(1)}, bf16[272,1024]{1,0:T(8,128)(2,1)S(1)}, u32[]{:S(2)}, u32[]{:S(2)}) collective-permute-start(bf16[272,1024]{1,0:T(8,128)(2,1)S(1)} %get-tuple-element.25.refs_0_.refs_3_.refs_5_.refs_7_.refs_8_), channel_id=1, source_target_pairs={{0,16},{8,24},{16,32},{24,40},{32,48},{40,56},{48,64},{56,72},{64,... | collective-permute-start | bytes 1671176 | tf_op jit(solution)/shard_map/ppermute | solution.py:171
  60.1 8.7 %collective-permute-done.1.refs_2_ = bf16[272,1024]{1,0:T(8,128)(2,1)S(1)} collective-permute-done((bf16[272,1024]{1,0:T(8,128)(2,1)S(1)}, bf16[272,1024]{1,0:T(8,128)(2,1)S(1)}, u32[]{:S(2)}, u32[]{:S(2)}) %collective-permute-start.1) | collective-permute-done | bytes 557088 | tf_op jit(solution)/shard_map/ppermute | solution.py:172
  68.8 5.6 %collective-permute-start.3 = (bf16[272,1024]{1,0:T(8,128)(2,1)S(1)}, bf16[272,1024]{1,0:T(8,128)(2,1)S(1)}, u32[]{:S(2)}, u32[]{:S(2)}) collective-permute-start(bf16[272,1024]{1,0:T(8,128)(2,1)S(1)} %collective-permute-done.1.refs_2_), channel_id=1, source_target_pairs={{0,112},{8,120},{16,0},{24,8},{32,16},{40,24},{48,32},{56,40},{64,... | collective-permute-start | bytes 1671176 | tf_op jit(solution)/shard_map/ppermute | solution.py:172
  74.4 1.9 %collective-permute-start.12 = (bf16[272,1024]{1,0:T(8,128)(2,1)S(1)}, bf16[272,1024]{1,0:T(8,128)(2,1)S(1)}, u32[]{:S(2)}, u32[]{:S(2)}) collective-permute-start(bf16[272,1024]{1,0:T(8,128)(2,1)S(1)} %collective-permute-done.11.refs_10_.refs_12_.refs_13_), channel_id=1, source_target_pairs={{0,7},{1,0},{2,1},{3,2},{4,3},{5,4},{6,5},{7,6},{8,15},{9,8},{10,9... | collective-permute-start | bytes 1671176 | tf_op jit(solution)/shard_map/ppermute | solution.py:170
  76.3 3.9 %collective-permute-start.13 = (bf16[272,1024]{1,0:T(8,128)(2,1)S(1)}, bf16[272,1024]{1,0:T(8,128)(2,1)S(1)}, u32[]{:S(2)}, u32[]{:S(2)}) collective-permute-start(bf16[272,1024]{1,0:T(8,128)(2,1)S(1)} %collective-permute-done.9.refs_17_.refs_18_), channel_id=1, source_target_pairs={{0,1},{1,2},{2,3},{3,4},{4,5},{5,6},{6,7},{7,0},{8,9},{9,10},{10,1... | collective-permute-start | bytes 1671176 | tf_op jit(solution)/shard_map/ppermute | solution.py:169
  80.3 1.9 %collective-permute-start.15 = (bf16[272,1024]{1,0:T(8,128)(2,1)S(1)}, bf16[272,1024]{1,0:T(8,128)(2,1)}, u32[]{:S(2)}, u32[]{:S(2)}) collective-permute-start(bf16[272,1024]{1,0:T(8,128)(2,1)S(1)} %get-tuple-element.25.refs_0_.refs_3_.refs_5_.refs_7_.refs_8_), channel_id=1, source_target_pairs={{0,8},{8,0},{16,24},{24,16},{32,40},{40,32},{48,56},{56,48},{64,72... | collective-permute-start | bytes 1671176 | tf_op jit(solution)/shard_map/ppermute | solution.py:168
  82.2 3.9 %collective-permute-done.3.refs_4_ = bf16[272,1024]{1,0:T(8,128)(2,1)S(1)} collective-permute-done((bf16[272,1024]{1,0:T(8,128)(2,1)S(1)}, bf16[272,1024]{1,0:T(8,128)(2,1)S(1)}, u32[]{:S(2)}, u32[]{:S(2)}) %collective-permute-start.3) | collective-permute-done | bytes 557088 | tf_op jit(solution)/shard_map/ppermute | solution.py:172
  86.1 1.9 %collective-permute-start.2 = (bf16[272,1024]{1,0:T(8,128)(2,1)S(1)}, bf16[272,1024]{1,0:T(8,128)(2,1)}, u32[]{:S(2)}, u32[]{:S(2)}) collective-permute-start(bf16[272,1024]{1,0:T(8,128)(2,1)S(1)} %collective-permute-done.refs_1_), channel_id=1, source_target_pairs={{0,16},{8,24},{16,32},{24,40},{32,48},{40,56},{48,64},{56,72},{64,... | collective-permute-start | bytes 1671176 | tf_op jit(solution)/shard_map/ppermute | solution.py:171
  88.0 2.2 %collective-permute-done.12.refs_18_.refs_19_ = bf16[272,1024]{1,0:T(8,128)(2,1)S(1)} collective-permute-done((bf16[272,1024]{1,0:T(8,128)(2,1)S(1)}, bf16[272,1024]{1,0:T(8,128)(2,1)S(1)}, u32[]{:S(2)}, u32[]{:S(2)}) %collective-permute-start.12) | collective-permute-done | bytes 557088 | tf_op jit(solution)/shard_map/ppermute | solution.py:170
  90.3 3.4 %collective-permute-start.5 = (bf16[272,1024]{1,0:T(8,128)(2,1)S(1)}, bf16[272,1024]{1,0:T(8,128)(2,1)}, u32[]{:S(2)}, u32[]{:S(2)}) collective-permute-start(bf16[272,1024]{1,0:T(8,128)(2,1)S(1)} %collective-permute-done.3.refs_4_), channel_id=1, source_target_pairs={{0,112},{8,120},{16,0},{24,8},{32,16},{40,24},{48,32},{56,40},{64,... | collective-permute-start | bytes 1671176 | tf_op jit(solution)/shard_map/ppermute | solution.py:172
  95.1 1.9 %collective-permute-start.14 = (bf16[816,1024]{1,0:T(8,128)(2,1)}, bf16[816,1024]{1,0:T(8,128)(2,1)}, u32[]{:S(2)}, u32[]{:S(2)}) collective-permute-start(bf16[816,1024]{1,0:T(8,128)(2,1)} %pad_maximum_fusion.1), channel_id=1, source_target_pairs={{0,8},{8,0},{16,24},{24,16},{32,40},{40,32},{48,56},{56,48},{64,72... | collective-permute-start | bytes 5013512 | tf_op jit(solution)/shard_map/ppermute | solution.py:168
  97.0 4.0 %shard_map.38 = (f32[3,8,256]{2,1,0:T(8,128)S(1)}, f32[256,256]{1,0:T(8,128)S(1)}, f32[256,256]{1,0:T(8,128)S(1)}, f32[256,256]{1,0:T(8,128)S(1)}, f32[256,256]{1,0:T(8,128)S(1)}) custom-call(bf16[272,1024]{1,0:T(8,128)(2,1)S(1)} %get-tuple-element.25.refs_0_.refs_3_.refs_5_.refs_7_.refs_8_, bf16[272,1024]{1,0:T(8,128)(2,1)S(1)} %collective-permute-done.refs_1_, ...), custom_call_target="tpu_custom_call" | custom-call | flops 1610612736 | bytes 3899392 | tf_op jit(solution)/shard_map/pallas_call | solution.py:125
  101.0 2.4 %collective-permute-done.2.refs_3_ = bf16[272,1024]{1,0:T(8,128)(2,1)} collective-permute-done((bf16[272,1024]{1,0:T(8,128)(2,1)S(1)}, bf16[272,1024]{1,0:T(8,128)(2,1)}, u32[]{:S(2)}, u32[]{:S(2)}) %collective-permute-start.2) | collective-permute-done | bytes 557088 | tf_op jit(solution)/shard_map/ppermute | solution.py:171
  103.4 1.9 %collective-permute-start.4 = (bf16[272,1024]{1,0:T(8,128)(2,1)}, bf16[272,1024]{1,0:T(8,128)(2,1)S(1)}, u32[]{:S(2)}, u32[]{:S(2)}) collective-permute-start(bf16[272,1024]{1,0:T(8,128)(2,1)} %collective-permute-done.2.refs_3_), channel_id=1, source_target_pairs={{0,16},{8,24},{16,32},{24,40},{32,48},{40,56},{48,64},{56,72},{64,... | collective-permute-start | bytes 1671176 | tf_op jit(solution)/shard_map/ppermute | solution.py:171
  105.4 5.8 %shard_map.39 = (f32[5,8,256]{2,1,0:T(8,128)S(1)}, f32[256,256]{1,0:T(8,128)S(1)}, f32[256,256]{1,0:T(8,128)S(1)}) custom-call(bf16[272,1024]{1,0:T(8,128)(2,1)S(1)} %get-tuple-element.25.refs_0_.refs_3_.refs_5_.refs_7_.refs_8_, bf16[272,1024]{1,0:T(8,128)(2,1)S(1)} %collective-permute-done.refs_1_, bf16[272,1024]{1,0:T(8,128)(2,1)S(1)} %collective-permute-done.1.refs_2_, ...), custom_call_target="tpu_custom_call" | custom-call | flops 2415919104 | bytes 8912896 | tf_op jit(solution)/shard_map/pallas_call | solution.py:125
  111.2 5.3 %collective-permute-start.6 = (bf16[272,1024]{1,0:T(8,128)(2,1)}, bf16[272,1024]{1,0:T(8,128)(2,1)S(1)}, u32[]{:S(2)}, u32[]{:S(2)}) collective-permute-start(bf16[272,1024]{1,0:T(8,128)(2,1)} %collective-permute-done.5.refs_6_), channel_id=1, source_target_pairs={{0,112},{8,120},{16,0},{24,8},{32,16},{40,24},{48,32},{56,40},{64,... | collective-permute-start | bytes 1671176 | tf_op jit(solution)/shard_map/ppermute | solution.py:172
  118.4 6.1 %shard_map.40 = (f32[5,8,256]{2,1,0:T(8,128)S(1)}, f32[256,256]{1,0:T(8,128)S(1)}, f32[256,256]{1,0:T(8,128)S(1)}, f32[256,256]{1,0:T(8,128)S(1)}, f32[256,256]{1,0:T(8,128)S(1)}) custom-call(bf16[272,1024]{1,0:T(8,128)(2,1)S(1)} %get-tuple-element.25.refs_0_.refs_3_.refs_5_.refs_7_.refs_8_, bf16[272,1024]{1,0:T(8,128)(2,1)S(1)} %collective-permute-done.refs_1_, ...), custom_call_target="tpu_custom_call" | custom-call | flops 2684354560 | bytes 5570560 | tf_op jit(solution)/shard_map/pallas_call | solution.py:125
  125.3 10.4 %shard_map.41 = (f32[7,8,256]{2,1,0:T(8,128)S(1)}, f32[256,256]{1,0:T(8,128)S(1)}, f32[256,256]{1,0:T(8,128)S(1)}) custom-call(bf16[272,1024]{1,0:T(8,128)(2,1)S(1)} %get-tuple-element.25.refs_0_.refs_3_.refs_5_.refs_7_.refs_8_, bf16[272,1024]{1,0:T(8,128)(2,1)S(1)} %collective-permute-done.refs_1_, bf16[272,1024]{1,0:T(8,128)(2,1)S(1)} %collective-permute-done.1.refs_2_, ...), custom_call_target="tpu_custom_call" | custom-call | flops 4563402752 | bytes 16711680 | tf_op jit(solution)/shard_map/pallas_call | solution.py:125
  136.6 9.0 %shard_map.42 = (f32[8,8,256]{2,1,0:T(8,128)S(1)}, f32[256,256]{1,0:T(8,128)}) custom-call(bf16[272,1024]{1,0:T(8,128)(2,1)S(1)} %get-tuple-element.25.refs_0_.refs_3_.refs_5_.refs_7_.refs_8_, bf16[272,1024]{1,0:T(8,128)(2,1)S(1)} %collective-permute-done.refs_1_, bf16[272,1024]{1,0:T(8,128)(2,1)S(1)} %collective-permute-done.1.refs_2_, ...), custom_call_target="tpu_custom_call" | custom-call | flops 2684354560 | bytes 18939904 | tf_op jit(solution)/shard_map/pallas_call | solution.py:125
  145.7 2.6 %fusion.1 = (bf16[272,1024]{1,0:T(8,128)(2,1)}, bf16[272,1024]{1,0:T(8,128)(2,1)}, bf16[272,1024]{1,0:T(8,128)(2,1)S(1)}) fusion(bf16[816,1024]{1,0:T(8,128)(2,1)} %collective-permute-done.14), kind=kLoop, calls=%fused_computation.4 | loop fusion | bytes 3342336 | tf_op jit(solution)/shard_map/slice | solution.py:187
  148.3 7.6 %shard_map.43 = (f32[8,8,256]{2,1,0:T(8,128)S(1)}, f32[256,256]{1,0:T(8,128)}, f32[256,256]{1,0:T(8,128)}, f32[256,256]{1,0:T(8,128)}) custom-call(bf16[272,1024]{1,0:T(8,128)(2,1)S(1)} %get-tuple-element.25.refs_0_.refs_3_.refs_5_.refs_7_.refs_8_, bf16[272,1024]{1,0:T(8,128)(2,1)S(1)} %collective-permute-done.refs_1_, ...), custom_call_target="tpu_custom_call" | custom-call | flops 3221225472 | bytes 6684672 | tf_op jit(solution)/shard_map/pallas_call | solution.py:125
  158.7 10.1 %all_to_all.9 = f32[8,1,256]{2,1,0:T(1,128)S(1)} all-to-all(f32[8,1,256]{2,1,0:T(1,128)S(1)} %copy.4), channel_id=1, replica_groups={{0,16,32,48,64,80,96,112},{8,24,40,56,72,88,104,120},{1,17,33,49,65,81,..., dimensions={0} | all-to-all | bytes 16384 | tf_op jit(solution)/shard_map/all_to_all | solution.py:211
  (60 shorter events, 12.5 us)
Async XLA Ops:
  2.6 17.2 %collective-permute-start.10 = (bf16[272,1024]{1,0:T(8,128)(2,1)S(1)}, bf16[272,1024]{1,0:T(8,128)(2,1)S(1)}, u32[]{:S(2)}, u32[]{:S(2)}) collective-permute-start(bf16[272,1024]{1,0:T(8,128)(2,1)S(1)} %get-tuple-element.25.refs_0_.refs_3_.refs_5_.refs_7_.refs_8_), channel_id=1, source_target_pairs={{0,7},{1,0},{2,1},{3,2},{4,3},{5,4},{6,5},{7,6},{8,15},{9,8},{10,9... | collective-permute-start | bytes 1671176 | tf_op jit(solution)/shard_map/ppermute | solution.py:170
  8.0 17.5 %collective-permute-start.7 = (bf16[272,1024]{1,0:T(8,128)(2,1)S(1)}, bf16[272,1024]{1,0:T(8,128)(2,1)S(1)}, u32[]{:S(2)}, u32[]{:S(2)}) collective-permute-start(bf16[272,1024]{1,0:T(8,128)(2,1)S(1)} %get-tuple-element.25.refs_0_.refs_3_.refs_5_.refs_7_.refs_8_), channel_id=1, source_target_pairs={{0,1},{1,2},{2,3},{3,4},{4,5},{5,6},{6,7},{7,0},{8,9},{9,10},{10,1... | collective-permute-start | bytes 1671176 | tf_op jit(solution)/shard_map/ppermute | solution.py:169
  19.9 85.5 %copy-start = (bf16[272,1024]{1,0:T(8,128)(2,1)}, bf16[272,1024]{1,0:T(8,128)(2,1)S(1)}, u32[]{:S(2)}) copy-start(bf16[272,1024]{1,0:T(8,128)(2,1)S(1)} %collective-permute-done.10.refs_6_.refs_8_.refs_10_.refs_11_) | copy-start | bytes 1671172
  19.9 16.6 %collective-permute-start.11 = (bf16[272,1024]{1,0:T(8,128)(2,1)S(1)}, bf16[272,1024]{1,0:T(8,128)(2,1)S(1)}, u32[]{:S(2)}, u32[]{:S(2)}) collective-permute-start(bf16[272,1024]{1,0:T(8,128)(2,1)S(1)} %collective-permute-done.10.refs_6_.refs_8_.refs_10_.refs_11_), channel_id=1, source_target_pairs={{0,7},{1,0},{2,1},{3,2},{4,3},{5,4},{6,5},{7,6},{8,15},{9,8},{10,9... | collective-permute-start | bytes 1671176 | tf_op jit(solution)/shard_map/ppermute | solution.py:170
  25.5 79.9 %copy-start.1 = (bf16[272,1024]{1,0:T(8,128)(2,1)}, bf16[272,1024]{1,0:T(8,128)(2,1)S(1)}, u32[]{:S(2)}) copy-start(bf16[272,1024]{1,0:T(8,128)(2,1)S(1)} %collective-permute-done.7.refs_5_.refs_7_.refs_9_.refs_10_) | copy-start | bytes 1671172
  25.5 16.3 %collective-permute-start.8 = (bf16[272,1024]{1,0:T(8,128)(2,1)S(1)}, bf16[272,1024]{1,0:T(8,128)(2,1)S(1)}, u32[]{:S(2)}, u32[]{:S(2)}) collective-permute-start(bf16[272,1024]{1,0:T(8,128)(2,1)S(1)} %collective-permute-done.7.refs_5_.refs_7_.refs_9_.refs_10_), channel_id=1, source_target_pairs={{0,1},{1,2},{2,3},{3,4},{4,5},{5,6},{6,7},{7,0},{8,9},{9,10},{10,1... | collective-permute-start | bytes 1671176 | tf_op jit(solution)/shard_map/ppermute | solution.py:169
  36.5 37.9 %copy-start.16 = (bf16[272,1024]{1,0:T(8,128)(2,1)}, bf16[272,1024]{1,0:T(8,128)(2,1)S(1)}, u32[]{:S(2)}) copy-start(bf16[272,1024]{1,0:T(8,128)(2,1)S(1)} %collective-permute-done.11.refs_10_.refs_12_.refs_13_) | copy-start | bytes 1671172
  41.8 14.4 %copy-start.17 = (bf16[272,1024]{1,0:T(8,128)(2,1)}, bf16[272,1024]{1,0:T(8,128)(2,1)S(1)}, u32[]{:S(2)}) copy-start(bf16[272,1024]{1,0:T(8,128)(2,1)S(1)} %collective-permute-done.8.refs_9_.refs_11_.refs_12_) | copy-start | bytes 1671172
  43.4 73.1 %collective-permute-start.16 = (bf16[1088,1024]{1,0:T(8,128)(2,1)}, bf16[1088,1024]{1,0:T(8,128)(2,1)}, u32[]{:S(2)}, u32[]{:S(2)}) collective-permute-start(bf16[1088,1024]{1,0:T(8,128)(2,1)} %pad_maximum_fusion), channel_id=1, source_target_pairs={{0,8},{8,0},{16,24},{24,16},{32,40},{40,32},{48,56},{56,48},{64,72... | collective-permute-start | bytes 6684680 | tf_op jit(solution)/shard_map/ppermute | solution.py:168
  45.3 23.5 %collective-permute-start.1 = (bf16[272,1024]{1,0:T(8,128)(2,1)S(1)}, bf16[272,1024]{1,0:T(8,128)(2,1)S(1)}, u32[]{:S(2)}, u32[]{:S(2)}) collective-permute-start(bf16[272,1024]{1,0:T(8,128)(2,1)S(1)} %get-tuple-element.25.refs_0_.refs_3_.refs_5_.refs_7_.refs_8_), channel_id=1, source_target_pairs={{0,112},{8,120},{16,0},{24,8},{32,16},{40,24},{48,32},{56,40},{64,... | collective-permute-start | bytes 1671176 | tf_op jit(solution)/shard_map/ppermute | solution.py:172
  56.3 20.1 %collective-permute-start.9 = (bf16[272,1024]{1,0:T(8,128)(2,1)S(1)}, bf16[272,1024]{1,0:T(8,128)(2,1)S(1)}, u32[]{:S(2)}, u32[]{:S(2)}) collective-permute-start(bf16[272,1024]{1,0:T(8,128)(2,1)S(1)} %collective-permute-done.8.refs_9_.refs_11_.refs_12_), channel_id=1, source_target_pairs={{0,1},{1,2},{2,3},{3,4},{4,5},{5,6},{6,7},{7,0},{8,9},{9,10},{10,1... | collective-permute-start | bytes 1671176 | tf_op jit(solution)/shard_map/ppermute | solution.py:169
  58.2 22.1 %collective-permute-start = (bf16[272,1024]{1,0:T(8,128)(2,1)S(1)}, bf16[272,1024]{1,0:T(8,128)(2,1)S(1)}, u32[]{:S(2)}, u32[]{:S(2)}) collective-permute-start(bf16[272,1024]{1,0:T(8,128)(2,1)S(1)} %get-tuple-element.25.refs_0_.refs_3_.refs_5_.refs_7_.refs_8_), channel_id=1, source_target_pairs={{0,16},{8,24},{16,32},{24,40},{32,48},{40,56},{48,64},{56,72},{64,... | collective-permute-start | bytes 1671176 | tf_op jit(solution)/shard_map/ppermute | solution.py:171
  68.8 17.3 %collective-permute-start.3 = (bf16[272,1024]{1,0:T(8,128)(2,1)S(1)}, bf16[272,1024]{1,0:T(8,128)(2,1)S(1)}, u32[]{:S(2)}, u32[]{:S(2)}) collective-permute-start(bf16[272,1024]{1,0:T(8,128)(2,1)S(1)} %collective-permute-done.1.refs_2_), channel_id=1, source_target_pairs={{0,112},{8,120},{16,0},{24,8},{32,16},{40,24},{48,32},{56,40},{64,... | collective-permute-start | bytes 1671176 | tf_op jit(solution)/shard_map/ppermute | solution.py:172
  74.4 15.9 %collective-permute-start.12 = (bf16[272,1024]{1,0:T(8,128)(2,1)S(1)}, bf16[272,1024]{1,0:T(8,128)(2,1)S(1)}, u32[]{:S(2)}, u32[]{:S(2)}) collective-permute-start(bf16[272,1024]{1,0:T(8,128)(2,1)S(1)} %collective-permute-done.11.refs_10_.refs_12_.refs_13_), channel_id=1, source_target_pairs={{0,7},{1,0},{2,1},{3,2},{4,3},{5,4},{6,5},{7,6},{8,15},{9,8},{10,9... | collective-permute-start | bytes 1671176 | tf_op jit(solution)/shard_map/ppermute | solution.py:170
  76.3 17.4 %copy-start.18 = (bf16[272,1024]{1,0:T(8,128)(2,1)}, bf16[272,1024]{1,0:T(8,128)(2,1)S(1)}, u32[]{:S(2)}) copy-start(bf16[272,1024]{1,0:T(8,128)(2,1)S(1)} %collective-permute-done.9.refs_17_.refs_18_) | copy-start | bytes 1671172
  76.3 17.3 %collective-permute-start.13 = (bf16[272,1024]{1,0:T(8,128)(2,1)S(1)}, bf16[272,1024]{1,0:T(8,128)(2,1)S(1)}, u32[]{:S(2)}, u32[]{:S(2)}) collective-permute-start(bf16[272,1024]{1,0:T(8,128)(2,1)S(1)} %collective-permute-done.9.refs_17_.refs_18_), channel_id=1, source_target_pairs={{0,1},{1,2},{2,3},{3,4},{4,5},{5,6},{6,7},{7,0},{8,9},{9,10},{10,1... | collective-permute-start | bytes 1671176 | tf_op jit(solution)/shard_map/ppermute | solution.py:169
  80.3 16.7 %collective-permute-start.15 = (bf16[272,1024]{1,0:T(8,128)(2,1)S(1)}, bf16[272,1024]{1,0:T(8,128)(2,1)}, u32[]{:S(2)}, u32[]{:S(2)}) collective-permute-start(bf16[272,1024]{1,0:T(8,128)(2,1)S(1)} %get-tuple-element.25.refs_0_.refs_3_.refs_5_.refs_7_.refs_8_), channel_id=1, source_target_pairs={{0,8},{8,0},{16,24},{24,16},{32,40},{40,32},{48,56},{56,48},{64,72... | collective-permute-start | bytes 1671176 | tf_op jit(solution)/shard_map/ppermute | solution.py:168
  86.1 38.4 %copy-start.6 = (bf16[272,1024]{1,0:T(8,128)(2,1)}, bf16[272,1024]{1,0:T(8,128)(2,1)S(1)}, u32[]{:S(2)}) copy-start(bf16[272,1024]{1,0:T(8,128)(2,1)S(1)} %collective-permute-done.3.refs_4_) | copy-start | bytes 1671172
  86.1 17.3 %collective-permute-start.2 = (bf16[272,1024]{1,0:T(8,128)(2,1)S(1)}, bf16[272,1024]{1,0:T(8,128)(2,1)}, u32[]{:S(2)}, u32[]{:S(2)}) collective-permute-start(bf16[272,1024]{1,0:T(8,128)(2,1)S(1)} %collective-permute-done.refs_1_), channel_id=1, source_target_pairs={{0,16},{8,24},{16,32},{24,40},{32,48},{40,56},{48,64},{56,72},{64,... | collective-permute-start | bytes 1671176 | tf_op jit(solution)/shard_map/ppermute | solution.py:171
  90.3 4.8 %copy-start.19 = (bf16[272,1024]{1,0:T(8,128)(2,1)}, bf16[272,1024]{1,0:T(8,128)(2,1)S(1)}, u32[]{:S(2)}) copy-start(bf16[272,1024]{1,0:T(8,128)(2,1)S(1)} %collective-permute-done.12.refs_18_.refs_19_) | copy-start | bytes 1671172
  90.3 20.9 %collective-permute-start.5 = (bf16[272,1024]{1,0:T(8,128)(2,1)S(1)}, bf16[272,1024]{1,0:T(8,128)(2,1)}, u32[]{:S(2)}, u32[]{:S(2)}) collective-permute-start(bf16[272,1024]{1,0:T(8,128)(2,1)S(1)} %collective-permute-done.3.refs_4_), channel_id=1, source_target_pairs={{0,112},{8,120},{16,0},{24,8},{32,16},{40,24},{48,32},{56,40},{64,... | collective-permute-start | bytes 1671176 | tf_op jit(solution)/shard_map/ppermute | solution.py:172
  93.7 3.3 %copy-start.20 = (bf16[272,1024]{1,0:T(8,128)(2,1)}, bf16[272,1024]{1,0:T(8,128)(2,1)S(1)}, u32[]{:S(2)}) copy-start(bf16[272,1024]{1,0:T(8,128)(2,1)S(1)} %collective-permute-done.13.refs_20_) | copy-start | bytes 1671172
  95.1 50.6 %collective-permute-start.14 = (bf16[816,1024]{1,0:T(8,128)(2,1)}, bf16[816,1024]{1,0:T(8,128)(2,1)}, u32[]{:S(2)}, u32[]{:S(2)}) collective-permute-start(bf16[816,1024]{1,0:T(8,128)(2,1)} %pad_maximum_fusion.1), channel_id=1, source_target_pairs={{0,8},{8,0},{16,24},{24,16},{32,40},{40,32},{48,56},{56,48},{64,72... | collective-permute-start | bytes 5013512 | tf_op jit(solution)/shard_map/ppermute | solution.py:168
  103.4 21.1 %collective-permute-start.4 = (bf16[272,1024]{1,0:T(8,128)(2,1)}, bf16[272,1024]{1,0:T(8,128)(2,1)S(1)}, u32[]{:S(2)}, u32[]{:S(2)}) collective-permute-start(bf16[272,1024]{1,0:T(8,128)(2,1)} %collective-permute-done.2.refs_3_), channel_id=1, source_target_pairs={{0,16},{8,24},{16,32},{24,40},{32,48},{40,56},{48,64},{56,72},{64,... | collective-permute-start | bytes 1671176 | tf_op jit(solution)/shard_map/ppermute | solution.py:171
  111.2 24.6 %collective-permute-start.6 = (bf16[272,1024]{1,0:T(8,128)(2,1)}, bf16[272,1024]{1,0:T(8,128)(2,1)S(1)}, u32[]{:S(2)}, u32[]{:S(2)}) collective-permute-start(bf16[272,1024]{1,0:T(8,128)(2,1)} %collective-permute-done.5.refs_6_), channel_id=1, source_target_pairs={{0,112},{8,120},{16,0},{24,8},{32,16},{40,24},{48,32},{56,40},{64,... | collective-permute-start | bytes 1671176 | tf_op jit(solution)/shard_map/ppermute | solution.py:172
  118.4 6.1 %copy-start.2 = (bf16[272,1024]{1,0:T(8,128)(2,1)}, bf16[272,1024]{1,0:T(8,128)(2,1)S(1)}, u32[]{:S(2)}) copy-start(bf16[272,1024]{1,0:T(8,128)(2,1)S(1)} %get-tuple-element.45.refs_8_.refs_16_.refs_17_) | copy-start | bytes 1671172
  118.4 6.1 %copy-start.3 = (bf16[272,1024]{1,0:T(8,128)(2,1)}, bf16[272,1024]{1,0:T(8,128)(2,1)S(1)}, u32[]{:S(2)}) copy-start(bf16[272,1024]{1,0:T(8,128)(2,1)S(1)} %get-tuple-element.46.refs_7_.refs_15_.refs_16_) | copy-start | bytes 1671172
  118.4 6.1 %copy-start.4 = (bf16[272,1024]{1,0:T(8,128)(2,1)}, bf16[272,1024]{1,0:T(8,128)(2,1)S(1)}, u32[]{:S(2)}) copy-start(bf16[272,1024]{1,0:T(8,128)(2,1)S(1)} %get-tuple-element.47.refs_6_.refs_14_.refs_15_) | copy-start | bytes 1671172
  118.4 6.1 %copy-start.5 = (bf16[272,1024]{1,0:T(8,128)(2,1)}, bf16[272,1024]{1,0:T(8,128)(2,1)S(1)}, u32[]{:S(2)}) copy-start(bf16[272,1024]{1,0:T(8,128)(2,1)S(1)} %get-tuple-element.48.refs_5_.refs_13_.refs_14_) | copy-start | bytes 1671172
  145.6 2.7 %copy-start.7 = (bf16[272,1024]{1,0:T(8,128)(2,1)S(1)}, bf16[272,1024]{1,0:T(8,128)(2,1)}, u32[]{:S(2)}) copy-start(bf16[272,1024]{1,0:T(8,128)(2,1)} %copy-done.6) | copy-start | bytes 1671172
  145.6 2.7 %copy-start.9 = (bf16[272,1024]{1,0:T(8,128)(2,1)S(1)}, bf16[272,1024]{1,0:T(8,128)(2,1)}, u32[]{:S(2)}) copy-start(bf16[272,1024]{1,0:T(8,128)(2,1)} %copy-done.8) | copy-start | bytes 1671172
  145.6 2.6 %copy-start.11 = (bf16[272,1024]{1,0:T(8,128)(2,1)S(1)}, bf16[272,1024]{1,0:T(8,128)(2,1)}, u32[]{:S(2)}) copy-start(bf16[272,1024]{1,0:T(8,128)(2,1)} %copy-done.10) | copy-start | bytes 1671172
  (6 other events, 4.7 us)

commit v2 on v0

v2 whole, which is shorter than its diff:
```python
import functools

import jax
import jax.numpy as jnp
from jax import lax
from jax.experimental import pallas as pl
from jax.experimental.pallas import tpu as pltpu
from jax.sharding import PartitionSpec as P

ROWS = 256
CLUSTERS = 16
SLOTS = 32
WINDOW = 48
ORDERS = 32768.0
LOW = -1e30
MIB = 1024 * 1024
META = 16
AUG = ROWS + META
START = 7


def iota(shape, dimension):
    return lax.broadcasted_iota(jnp.int32, shape, dimension)


def turn(line):
    return jnp.concatenate([jnp.broadcast_to(line[:, h : h + 128], (128, 128)).T for h in (0, 128)], axis=0)


def tall(meta):
    filled = jnp.concatenate([meta, jnp.zeros((128 - META, ROWS), meta.dtype)], axis=0)
    return jnp.concatenate([filled[:, 0:128].T, filled[:, 128:256].T], axis=0)


def prepare_kernel(x_ref, cluster_ref, order_ref, aug_ref, norm_ref, slot_ref):
    rows = x_ref[...]
    wide = rows.astype(jnp.float32)
    norm = jnp.broadcast_to(lax.rsqrt(jnp.sum(wide * wide, axis=1, keepdims=True) + 1e-06), (ROWS, 128))
    norm = jnp.concatenate([norm[0:128, :].T[0:1, :], norm[128:256, :].T[0:1, :]], axis=1)
    cluster = cluster_ref[...].astype(jnp.float32)
    order = order_ref[...]
    floor = cluster * ORDERS
    key = floor + order.astype(jnp.float32)
    key_down = jnp.concatenate([turn(key)] * 2, axis=1)
    rank = jnp.sum((key_down < key).astype(jnp.float32), axis=0, keepdims=True)
    inside = rank - jnp.sum((key_down < floor).astype(jnp.float32), axis=0, keepdims=True)
    high = jnp.right_shift(order, 8).astype(jnp.float32)
    low = jnp.bitwise_and(order, 255).astype(jnp.float32)
    first = norm.astype(jnp.bfloat16).astype(jnp.float32)
    second = (norm - first).astype(jnp.bfloat16).astype(jnp.float32)
    third = norm - first - second

    line, lane = iota((META, ROWS), 0), iota((META, ROWS), 1)
    meta = jnp.zeros((META, ROWS), jnp.float32)
    for index, values in enumerate((cluster, high, low, first, second, third, inside)):
        meta = jnp.where(line == index, values, meta)
    permute = (iota((ROWS, ROWS), 0).astype(jnp.float32) == rank).astype(jnp.bfloat16)
    meta = by_lines(meta.astype(jnp.bfloat16), permute)
    count = jnp.sum((turn(cluster) < iota((ROWS, 128), 1).astype(jnp.float32)).astype(jnp.float32), axis=0, keepdims=True)
    start = jnp.minimum(jnp.bitwise_and(count.astype(jnp.int32), -16), ROWS - WINDOW).astype(jnp.float32)
    meta = jnp.where(line == START, jnp.concatenate([start] * 2, axis=1), meta)

    aug_ref[0:ROWS, :] = jnp.dot(permute, rows, preferred_element_type=jnp.float32).astype(jnp.bfloat16)
    aug_ref[ROWS:AUG, :] = jnp.zeros((META, rows.shape[1]), jnp.bfloat16)
    aug_ref[ROWS:AUG, 0:ROWS] = meta.astype(jnp.bfloat16)
    norm_ref[...] = norm
    slot_ref[...] = cluster * float(SLOTS) + inside


def prepare(x, cluster, order):
    return pl.pallas_call(
        prepare_kernel,
        out_shape=(
            jax.ShapeDtypeStruct((AUG, x.shape[1]), jnp.bfloat16),
            jax.ShapeDtypeStruct((1, ROWS), jnp.float32),
            jax.ShapeDtypeStruct((1, ROWS), jnp.float32),
        ),
        compiler_params=pltpu.CompilerParams(vmem_limit_bytes=16 * MIB),
    )(x, cluster.reshape(1, ROWS), order.reshape(1, ROWS))


def line_weights():
    line, lane = iota((16, 128), 0), iota((16, 128), 1)
    weights = jnp.zeros((16, 128), jnp.float32)
    for at, of, weight in ((0, 0, ORDERS), (0, 1, 256.0), (0, 2, 1.0), (1, 0, ORDERS)):
        weights = jnp.where((line == at) & (lane == of), weight, weights)
    return weights.astype(jnp.bfloat16)


def spread_weights():
    line, lane = iota((128, 256), 0), iota((128, 256), 1)
    weights = jnp.zeros((128, 256), jnp.float32)
    for of, weight in ((0, ORDERS), (1, 256.0), (2, 1.0)):
        weights = jnp.where((line == of) & (lane < 128), weight, weights)
    return jnp.where((line >= 3) & (line <= 5) & (lane >= 128), 1.0, weights).astype(jnp.bfloat16)


def by_lines(weights, meta):
    return lax.dot_general(weights, meta, (((1,), (1,)), ((), ())), preferred_element_type=jnp.float32)


def match_kernel(offsets, table_ref, place_ref, *refs):
    rows = refs[: len(offsets)]
    cols_ref, out_ref, held, held_meta, slots, slot_meta, sem = refs[len(offsets) :]
    blocks = cols_ref.shape[0] // AUG
    width = held.shape[2]
    copies = [
        pltpu.make_async_copy(cols_ref.at[b * AUG : (b + 1) * AUG, :], held.at[b], sem.at[b]) for b in range(blocks)
    ]
    for copy in copies:
        copy.start()
    for ref, offset in zip(rows, offsets):
        meta = ref[ROWS:AUG, 0:ROWS]
        wide = meta.astype(jnp.float32)
        slot = wide[0:1] * float(SLOTS) + wide[6:7]
        pick = (iota((CLUSTERS * SLOTS, ROWS), 0).astype(jnp.float32) == slot).astype(jnp.bfloat16)
        home = pl.multiple_of(lax.rem(place_ref[0] + offset, 8) * SLOTS, SLOTS)
        spread = jnp.dot(pick, ref[0:ROWS, :], preferred_element_type=jnp.float32).astype(jnp.bfloat16)
        slots[:, pl.ds(home, SLOTS), :] = spread.reshape(CLUSTERS, SLOTS, width)
        spread = jnp.dot(pick, tall(meta), preferred_element_type=jnp.float32).astype(jnp.bfloat16)
        slot_meta[:, pl.ds(home, SLOTS), :] = spread.reshape(CLUSTERS, SLOTS, 128)
    for b, copy in enumerate(copies):
        copy.wait()
        held_meta[b] = tall(held[b, ROWS:AUG, 0:ROWS])
    groups = blocks * WINDOW // 8

    def cluster(g, carry):
        starts = [pl.multiple_of(table_ref[b, g], 16) for b in range(blocks)]
        window = jnp.concatenate([held[b, pl.ds(starts[b], WINDOW), :] for b in range(blocks)], axis=0)
        window_meta = jnp.concatenate([held_meta[b, pl.ds(starts[b], WINDOW), :] for b in range(blocks)], axis=0)
        score = lax.dot_general(
            window, slots[g], (((1,), (1,)), ((), ())), preferred_element_type=jnp.float32
        )
        col = jnp.dot(window_meta, spread_weights(), preferred_element_type=jnp.float32)
        row = by_lines(line_weights(), slot_meta[g])
        key = col[:, 0:128].reshape(groups, 8, 128)
        norm = col[:, 128:256].reshape(groups, 8, 128)
        halves = []
        for half in (0, 128):
            row_key, row_floor = row[0:1, half : half + 128], row[1:2, half : half + 128]
            valid = (key < row_key) & (key >= row_floor)
            scaled = score[:, half : half + 128].reshape(groups, 8, 128) * norm
            halves.append(jnp.max(jnp.where(valid, scaled, LOW), axis=0))
        best = jnp.concatenate(halves, axis=1)
        out_ref[g] = jnp.max(best, axis=0, keepdims=True)
        return carry

    lax.fori_loop(0, CLUSTERS, cluster, 0, unroll=UNROLL)


UNROLL = 2


def match(table, place, rows, offsets, cols):
    width = cols.shape[1]
    blocks = cols.shape[0] // AUG
    vmem, smem = pl.BlockSpec(memory_space=pltpu.VMEM), pl.BlockSpec(memory_space=pltpu.SMEM)
    return pl.pallas_call(
        functools.partial(match_kernel, offsets),
        out_shape=jax.ShapeDtypeStruct((CLUSTERS, 1, 8 * SLOTS), jnp.float32),
        in_specs=[smem, smem] + [vmem] * len(rows) + [pl.BlockSpec(memory_space=pltpu.HBM)],
        out_specs=vmem,
        scratch_shapes=[
            pltpu.VMEM((blocks, AUG, width), jnp.bfloat16),
            pltpu.VMEM((blocks, ROWS, 128), jnp.bfloat16),
            pltpu.VMEM((CLUSTERS, 8 * SLOTS, width), jnp.bfloat16),
            pltpu.VMEM((CLUSTERS, 8 * SLOTS, 128), jnp.bfloat16),
            pltpu.SemaphoreType.DMA((blocks,)),
        ],
        compiler_params=pltpu.CompilerParams(vmem_limit_bytes=44 * MIB),
    )(table, place, *rows, cols)


def collect_kernel(found_ref, slot_ref, norm_ref, out_ref):
    found = jnp.max(found_ref[...], axis=0, keepdims=True)
    column = jnp.concatenate([turn(found[:, h : h + 256]) for h in (0, 256)], axis=0)
    for half in (0, 128):
        slot = slot_ref[:, half : half + 128]
        mine = iota((CLUSTERS * SLOTS, 128), 0).astype(jnp.float32) == slot
        best = jnp.max(jnp.where(mine, column, LOW), axis=0, keepdims=True)
        out_ref[:, half : half + 128] = jnp.maximum(best * norm_ref[:, half : half + 128], -1.0)


def collect(found, slot, norm):
    return pl.pallas_call(
        collect_kernel,
        out_shape=jax.ShapeDtypeStruct((1, ROWS), jnp.float32),
    )(found, slot, norm)


def ring(size, step):
    return [(i, (i + step) % size) for i in range(size)]


def per_device(embeddings, cluster_id, member_order):
    own, norm, slot = prepare(embeddings, cluster_id, member_order)
    cols = lax.all_gather(own, "grp", axis=0, tiled=True)
    tables = cols.reshape(16, AUG, embeddings.shape[1])[:, ROWS + START, 0:CLUSTERS].astype(jnp.int32)

    up = lambda v: lax.ppermute(v, "span", ring(8, 1))
    down = lambda v: lax.ppermute(v, "span", ring(8, -1))
    blocks, u, d = [own], own, own
    for _ in range(3):
        u, d = up(u), down(d)
        blocks += [u, d]
    blocks.append(up(u))
    place = lax.axis_index("span").astype(jnp.int32).reshape(1)
    found = match(tables, place, blocks, (0, 7, 1, 6, 2, 5, 3, 4), cols).reshape(CLUSTERS, 8, SLOTS)
    found = found.transpose(1, 0, 2).reshape(8, CLUSTERS * SLOTS)
    arrived = lax.all_to_all(found, "span", split_axis=0, concat_axis=0, tiled=True)
    return collect(arrived, slot, norm)[0]


def solution(mesh):
    return jax.shard_map(
        per_device,
        mesh=mesh,
        in_specs=(
            P(("outer", "grp", "span"), None),
            P(("outer", "grp", "span")),
            P(("outer", "grp", "span")),
        ),
        out_specs=P(("outer", "grp", "span")),
        check_vma=False,
    )
```

time: 188 us -> 122 us (0.65)
  the two profiles are of different devices: /device:TPU:1 before, /device:TPU:2 now
where the time goes in v2:
time: 122 us; the launch traced here: 121 us
  waiting for transfers between devices  43.3 us (35%)
  starting transfers between devices  23.3 us (19%)
  Pallas kernels  21.4 us (18%)
  blocking collectives  14.3 us (12%)
  between operations  13.5 us (11%)
  local copies, waits for them, and re-layouts  5.14 us (4%)
    ppermute x4, waiting for transfers between devices, per_device(): up = lambda v: lax.ppermute(v, 'span', ring(8, 1))  29.8 us
    pallas_call x1, Pallas kernels, match(): pl.pallas_call(functools.partial(match_kernel, offsets), out_shape=jax.Sh...  18.6 us
    all_to_all x1, blocking collectives, per_device(): lax.all_to_all(found, 'span', split_axis=0, concat_axis=0, tiled=True)  14.3 us
    ppermute x3, starting transfers between devices, per_device(): down = lambda v: lax.ppermute(v, 'span', ring(8, -1))  14.1 us
    all_gather x1, waiting for transfers between devices, per_device(): cols = lax.all_gather(own, 'grp', axis=0, tiled=True)  13.5 us
    ppermute x4, starting transfers between devices, per_device(): up = lambda v: lax.ppermute(v, 'span', ring(8, 1))  9.21 us
    unnamed x11, local copies, waits for them, and re-layouts  4.18 us
  transfers between devices with their start and end apart: 8, of which 4 were waited for; matrix products, arithmetic and copies ran while one was open for 1% of the time, Pallas kernels for 0%

profile of v2, /device:TPU:2, one launch (start us, length us, event | category | flops | bytes accessed | tf_op | source)
XLA Modules:
  0.0 121.0 jit_solution(13047482446393600949)
XLA Ops:
  6.5 0.0 all-gather.2.cloned.1.call-start
  6.5 0.0 copy-start
  6.5 1.0 copy-done
  7.6 0.0 copy-start.1
  7.6 0.7 copy-done.1
  8.3 0.7 copy-done.2
  8.9 1.3 %shard_map.37 = (bf16[272,1024]{1,0:T(8,128)(2,1)}, f32[1,256]{1,0:T(1,128)S(1)}, f32[1,256]{1,0:T(1,128)S(1)}) custom-call(bf16[256,1024]{1,0:T(8,128)(2,1)S(1)} %copy-done, s32[1,256]{1,0:T(1,128)S(1)} %bitcast.14, s32[1,256]{1,0:T(1,128)S(1)} %bitcast.15), custom_call_target="tpu_custom_call" | custom-call | tf_op jit(solution)/shard_map/pallas_call | solution.py:71
  10.3 0.6 copy-done.3
  10.9 0.6 copy-done.4
  11.5 0.0 all-gather.2.cloned.1.call-update
  11.5 3.5 %collective-permute-start = (bf16[272,1024]{1,0:T(8,128)(2,1)}, bf16[272,1024]{1,0:T(8,128)(2,1)S(1)}, u32[]{:S(2)}, u32[]{:S(2)}) collective-permute-start(bf16[272,1024]{1,0:T(8,128)(2,1)} %get-tuple-element.8.refs_0_), channel_id=1, source_target_pairs={{0,1},{1,2},{2,3},{3,4},{4,5},{5,6},{6,7},{7,0},{8,9},{9,10},{10,1... | collective-permute-start | bytes 1671176 | tf_op jit(solution)/shard_map/ppermute | solution.py:200
  15.0 3.8 %collective-permute-start.1 = (bf16[272,1024]{1,0:T(8,128)(2,1)}, bf16[272,1024]{1,0:T(8,128)(2,1)S(1)}, u32[]{:S(2)}, u32[]{:S(2)}) collective-permute-start(bf16[272,1024]{1,0:T(8,128)(2,1)} %get-tuple-element.8.refs_0_), channel_id=1, source_target_pairs={{0,7},{1,0},{2,1},{3,2},{4,3},{5,4},{6,5},{7,6},{8,15},{9,8},{10,9... | collective-permute-start | bytes 1671176 | tf_op jit(solution)/shard_map/ppermute | solution.py:201
  18.8 10.9 %collective-permute-done.refs_1_ = bf16[272,1024]{1,0:T(8,128)(2,1)S(1)} collective-permute-done((bf16[272,1024]{1,0:T(8,128)(2,1)}, bf16[272,1024]{1,0:T(8,128)(2,1)S(1)}, u32[]{:S(2)}, u32[]{:S(2)}) %collective-permute-start) | collective-permute-done | bytes 557088 | tf_op jit(solution)/shard_map/ppermute | solution.py:200
  29.7 1.9 %collective-permute-start.2 = (bf16[272,1024]{1,0:T(8,128)(2,1)S(1)}, bf16[272,1024]{1,0:T(8,128)(2,1)S(1)}, u32[]{:S(2)}, u32[]{:S(2)}) collective-permute-start(bf16[272,1024]{1,0:T(8,128)(2,1)S(1)} %collective-permute-done.refs_1_), channel_id=1, source_target_pairs={{0,1},{1,2},{2,3},{3,4},{4,5},{5,6},{6,7},{7,0},{8,9},{9,10},{10,1... | collective-permute-start | bytes 1671176 | tf_op jit(solution)/shard_map/ppermute | solution.py:200
  31.6 0.0 collective-permute-done.1.refs_2_
  31.6 5.1 %collective-permute-start.3 = (bf16[272,1024]{1,0:T(8,128)(2,1)S(1)}, bf16[272,1024]{1,0:T(8,128)(2,1)S(1)}, u32[]{:S(2)}, u32[]{:S(2)}) collective-permute-start(bf16[272,1024]{1,0:T(8,128)(2,1)S(1)} %collective-permute-done.1.refs_2_), channel_id=1, source_target_pairs={{0,7},{1,0},{2,1},{3,2},{4,3},{5,4},{6,5},{7,6},{8,15},{9,8},{10,9... | collective-permute-start | bytes 1671176 | tf_op jit(solution)/shard_map/ppermute | solution.py:201
  36.8 9.8 %collective-permute-done.2.refs_3_ = bf16[272,1024]{1,0:T(8,128)(2,1)S(1)} collective-permute-done((bf16[272,1024]{1,0:T(8,128)(2,1)S(1)}, bf16[272,1024]{1,0:T(8,128)(2,1)S(1)}, u32[]{:S(2)}, u32[]{:S(2)}) %collective-permute-start.2) | collective-permute-done | bytes 557088 | tf_op jit(solution)/shard_map/ppermute | solution.py:200
  46.6 1.9 %collective-permute-start.4 = (bf16[272,1024]{1,0:T(8,128)(2,1)S(1)}, bf16[272,1024]{1,0:T(8,128)(2,1)S(1)}, u32[]{:S(2)}, u32[]{:S(2)}) collective-permute-start(bf16[272,1024]{1,0:T(8,128)(2,1)S(1)} %collective-permute-done.2.refs_3_), channel_id=1, source_target_pairs={{0,1},{1,2},{2,3},{3,4},{4,5},{5,6},{6,7},{7,0},{8,9},{9,10},{10,1... | collective-permute-start | bytes 1671176 | tf_op jit(solution)/shard_map/ppermute | solution.py:200
  48.5 0.0 collective-permute-done.3.refs_4_
  48.5 5.1 %collective-permute-start.5 = (bf16[272,1024]{1,0:T(8,128)(2,1)S(1)}, bf16[272,1024]{1,0:T(8,128)(2,1)S(1)}, u32[]{:S(2)}, u32[]{:S(2)}) collective-permute-start(bf16[272,1024]{1,0:T(8,128)(2,1)S(1)} %collective-permute-done.3.refs_4_), channel_id=1, source_target_pairs={{0,7},{1,0},{2,1},{3,2},{4,3},{5,4},{6,5},{7,6},{8,15},{9,8},{10,9... | collective-permute-start | bytes 1671176 | tf_op jit(solution)/shard_map/ppermute | solution.py:201
  53.7 9.0 %collective-permute-done.4.refs_5_ = bf16[272,1024]{1,0:T(8,128)(2,1)S(1)} collective-permute-done((bf16[272,1024]{1,0:T(8,128)(2,1)S(1)}, bf16[272,1024]{1,0:T(8,128)(2,1)S(1)}, u32[]{:S(2)}, u32[]{:S(2)}) %collective-permute-start.4) | collective-permute-done | bytes 557088 | tf_op jit(solution)/shard_map/ppermute | solution.py:200
  62.7 1.9 %collective-permute-start.6 = (bf16[272,1024]{1,0:T(8,128)(2,1)S(1)}, bf16[272,1024]{1,0:T(8,128)(2,1)}, u32[]{:S(2)}, u32[]{:S(2)}) collective-permute-start(bf16[272,1024]{1,0:T(8,128)(2,1)S(1)} %collective-permute-done.4.refs_5_), channel_id=1, source_target_pairs={{0,1},{1,2},{2,3},{3,4},{4,5},{5,6},{6,7},{7,0},{8,9},{9,10},{10,1... | collective-permute-start | bytes 1671176 | tf_op jit(solution)/shard_map/ppermute | solution.py:200
  64.6 13.5 %all-gather.2.cloned.1.call-done.refs_8_ = bf16[4352,1024]{1,0:T(8,128)(2,1)} async-done(((bf16[272,1024]{1,0:T(8,128)(2,1)}), bf16[4352,1024]{1,0:T(8,128)(2,1)}) %all-gather.2.cloned.1.call-update) | async-done | bytes 8912912 | tf_op jit(solution)/shard_map/all_gather | solution.py:197
  78.1 0.8 slice.4
  78.9 0.0 collective-permute-done.5.refs_6_
  78.9 0.0 collective-permute-done.6.refs_7_
  78.9 18.6 %shard_map.38 = f32[16,1,256]{2,1,0:T(1,128)S(1)} custom-call(s32[16,16]{1,0:T(8,128)S(1)} %fusion.table_ref, s32[1]{0:T(128)} %bitcast.4.place_ref, bf16[272,1024]{1,0:T(8,128)(2,1)} %get-tuple-element.8.refs_0_, bf16[272,1024]{1,0:T(8,128)(2,1)S(1)} %collective-permute-done.refs_1_, bf16[272,1024]{1,0:T(8,128)(2,1)S(1)} %collective-permute-done.1.refs_2_, ...), custom_call_target="tpu_custom_call" | custom-call | tf_op jit(solution)/shard_map/pallas_call | solution.py:158
  97.6 0.1 reshape.25
  97.7 0.1 all_to_all.7
  97.8 14.3 %all_to_all.11 = f32[8,1,512]{2,1,0:T(1,128)S(1)} all-to-all(f32[8,1,512]{2,1,0:T(1,128)S(1)} %all_to_all.7), channel_id=1, replica_groups=mesh['outer'=4,'grp'=16,'span'=8] {'span'}, dimensions={0} | all-to-all | bytes 32768 | tf_op jit(solution)/shard_map/all_to_all | solution.py:210
  112.1 0.6 copy.14
  112.7 1.4 %shard_map.39 = f32[1,256]{1,0:T(1,128)} custom-call(f32[8,512]{1,0:T(8,128)} %bitcast.18, f32[1,256]{1,0:T(1,128)} %copy-done.4, f32[1,256]{1,0:T(1,128)} %copy-done.3), custom_call_target="tpu_custom_call" | custom-call | tf_op jit(solution)/shard_map/pallas_call | solution.py:185
  (6 shorter events, 0.1 us)
Async XLA Ops:
  6.5 71.6 %all-gather.2.cloned.1.call-start = ((), (), s32[]{:S(2)}) async-start(), calls=%async_computation.1 | async-start | bytes 9469952 | tf_op jit(solution)/shard_map/all_gather | solution.py:197
  6.5 1.0 copy-start
  7.6 0.7 copy-start.1
  8.3 0.7 copy-start.2
  10.3 0.6 copy-start.3
  10.9 0.6 copy-start.4
  11.5 18.2 %collective-permute-start = (bf16[272,1024]{1,0:T(8,128)(2,1)}, bf16[272,1024]{1,0:T(8,128)(2,1)S(1)}, u32[]{:S(2)}, u32[]{:S(2)}) collective-permute-start(bf16[272,1024]{1,0:T(8,128)(2,1)} %get-tuple-element.8.refs_0_), channel_id=1, source_target_pairs={{0,1},{1,2},{2,3},{3,4},{4,5},{5,6},{6,7},{7,0},{8,9},{9,10},{10,1... | collective-permute-start | bytes 1671176 | tf_op jit(solution)/shard_map/ppermute | solution.py:200
  15.0 16.6 %collective-permute-start.1 = (bf16[272,1024]{1,0:T(8,128)(2,1)}, bf16[272,1024]{1,0:T(8,128)(2,1)S(1)}, u32[]{:S(2)}, u32[]{:S(2)}) collective-permute-start(bf16[272,1024]{1,0:T(8,128)(2,1)} %get-tuple-element.8.refs_0_), channel_id=1, source_target_pairs={{0,7},{1,0},{2,1},{3,2},{4,3},{5,4},{6,5},{7,6},{8,15},{9,8},{10,9... | collective-permute-start | bytes 1671176 | tf_op jit(solution)/shard_map/ppermute | solution.py:201
  29.7 16.9 %collective-permute-start.2 = (bf16[272,1024]{1,0:T(8,128)(2,1)S(1)}, bf16[272,1024]{1,0:T(8,128)(2,1)S(1)}, u32[]{:S(2)}, u32[]{:S(2)}) collective-permute-start(bf16[272,1024]{1,0:T(8,128)(2,1)S(1)} %collective-permute-done.refs_1_), channel_id=1, source_target_pairs={{0,1},{1,2},{2,3},{3,4},{4,5},{5,6},{6,7},{7,0},{8,9},{9,10},{10,1... | collective-permute-start | bytes 1671176 | tf_op jit(solution)/shard_map/ppermute | solution.py:200
  31.6 16.9 %collective-permute-start.3 = (bf16[272,1024]{1,0:T(8,128)(2,1)S(1)}, bf16[272,1024]{1,0:T(8,128)(2,1)S(1)}, u32[]{:S(2)}, u32[]{:S(2)}) collective-permute-start(bf16[272,1024]{1,0:T(8,128)(2,1)S(1)} %collective-permute-done.1.refs_2_), channel_id=1, source_target_pairs={{0,7},{1,0},{2,1},{3,2},{4,3},{5,4},{6,5},{7,6},{8,15},{9,8},{10,9... | collective-permute-start | bytes 1671176 | tf_op jit(solution)/shard_map/ppermute | solution.py:201
  46.6 16.1 %collective-permute-start.4 = (bf16[272,1024]{1,0:T(8,128)(2,1)S(1)}, bf16[272,1024]{1,0:T(8,128)(2,1)S(1)}, u32[]{:S(2)}, u32[]{:S(2)}) collective-permute-start(bf16[272,1024]{1,0:T(8,128)(2,1)S(1)} %collective-permute-done.2.refs_3_), channel_id=1, source_target_pairs={{0,1},{1,2},{2,3},{3,4},{4,5},{5,6},{6,7},{7,0},{8,9},{9,10},{10,1... | collective-permute-start | bytes 1671176 | tf_op jit(solution)/shard_map/ppermute | solution.py:200
  48.5 30.4 %collective-permute-start.5 = (bf16[272,1024]{1,0:T(8,128)(2,1)S(1)}, bf16[272,1024]{1,0:T(8,128)(2,1)S(1)}, u32[]{:S(2)}, u32[]{:S(2)}) collective-permute-start(bf16[272,1024]{1,0:T(8,128)(2,1)S(1)} %collective-permute-done.3.refs_4_), channel_id=1, source_target_pairs={{0,7},{1,0},{2,1},{3,2},{4,3},{5,4},{6,5},{7,6},{8,15},{9,8},{10,9... | collective-permute-start | bytes 1671176 | tf_op jit(solution)/shard_map/ppermute | solution.py:201
  62.7 16.2 %collective-permute-start.6 = (bf16[272,1024]{1,0:T(8,128)(2,1)S(1)}, bf16[272,1024]{1,0:T(8,128)(2,1)}, u32[]{:S(2)}, u32[]{:S(2)}) collective-permute-start(bf16[272,1024]{1,0:T(8,128)(2,1)S(1)} %collective-permute-done.4.refs_5_), channel_id=1, source_target_pairs={{0,1},{1,2},{2,3},{3,4},{4,5},{5,6},{6,7},{7,0},{8,9},{9,10},{10,1... | collective-permute-start | bytes 1671176 | tf_op jit(solution)/shard_map/ppermute | solution.py:200
Sparse Core Ops, SparseCore 0:
  11.6 66.4 all-gather.1

commit v3 on v2

v3 whole, which is shorter than its diff:
```python
import functools

import jax
import jax.numpy as jnp
from jax import lax
from jax.experimental import pallas as pl
from jax.experimental.pallas import tpu as pltpu
from jax.sharding import PartitionSpec as P

ROWS = 256
CLUSTERS = 16
SLOTS = 32
WINDOW = 48
ORDERS = 32768.0
LOW = -1e30
MIB = 1024 * 1024
META = 16
AUG = ROWS + META
START = 7


def iota(shape, dimension):
    return lax.broadcasted_iota(jnp.int32, shape, dimension)


def turn(line):
    return jnp.concatenate([jnp.broadcast_to(line[:, h : h + 128], (128, 128)).T for h in (0, 128)], axis=0)


def tall(meta):
    filled = jnp.concatenate([meta, jnp.zeros((128 - META, ROWS), meta.dtype)], axis=0)
    return jnp.concatenate([filled[:, 0:128].T, filled[:, 128:256].T], axis=0)


def row_facts(rows, cluster, order):
    wide = rows.astype(jnp.float32)
    norm = jnp.broadcast_to(lax.rsqrt(jnp.sum(wide * wide, axis=1, keepdims=True) + 1e-06), (ROWS, 128))
    norm = jnp.concatenate([norm[0:128, :].T[0:1, :], norm[128:256, :].T[0:1, :]], axis=1)
    floor = cluster * ORDERS
    key = floor + order
    key_down = jnp.concatenate([turn(key)] * 2, axis=1)
    rank = jnp.sum((key_down < key).astype(jnp.float32), axis=0, keepdims=True)
    inside = rank - jnp.sum((key_down < floor).astype(jnp.float32), axis=0, keepdims=True)
    return norm, rank, inside


def staged(refs, held, sem):
    copies = [pltpu.make_async_copy(ref, to, sem.at[i]) for i, (ref, to) in enumerate(zip(refs, held))]
    for copy in copies:
        copy.start()
    for copy in copies:
        copy.wait()


def prepare_kernel(x_hbm, cluster_hbm, order_hbm, aug_ref, x_ref, cluster_ref, order_ref, sem):
    staged((x_hbm, cluster_hbm, order_hbm), (x_ref, cluster_ref, order_ref), sem)
    rows = x_ref[...]
    cluster = cluster_ref[...].astype(jnp.float32)
    order = order_ref[...]
    norm, rank, inside = row_facts(rows, cluster, order.astype(jnp.float32))
    high = jnp.right_shift(order, 8).astype(jnp.float32)
    low = jnp.bitwise_and(order, 255).astype(jnp.float32)
    first = norm.astype(jnp.bfloat16).astype(jnp.float32)
    second = (norm - first).astype(jnp.bfloat16).astype(jnp.float32)
    third = norm - first - second

    line = iota((META, ROWS), 0)
    meta = jnp.zeros((META, ROWS), jnp.float32)
    for index, values in enumerate((cluster, high, low, first, second, third, inside)):
        meta = jnp.where(line == index, values, meta)
    permute = (iota((ROWS, ROWS), 0).astype(jnp.float32) == rank).astype(jnp.bfloat16)
    meta = by_lines(meta.astype(jnp.bfloat16), permute)
    count = jnp.sum((turn(cluster) < iota((ROWS, 128), 1).astype(jnp.float32)).astype(jnp.float32), axis=0, keepdims=True)
    start = jnp.minimum(jnp.bitwise_and(count.astype(jnp.int32), -16), ROWS - WINDOW).astype(jnp.float32)
    meta = jnp.where(line == START, jnp.concatenate([start] * 2, axis=1), meta)

    aug_ref[0:ROWS, :] = jnp.dot(permute, rows, preferred_element_type=jnp.float32).astype(jnp.bfloat16)
    aug_ref[ROWS:AUG, :] = jnp.zeros((META, rows.shape[1]), jnp.bfloat16)
    aug_ref[ROWS:AUG, 0:ROWS] = meta.astype(jnp.bfloat16)


def remember_kernel(x_hbm, cluster_hbm, order_hbm, out_ref, x_ref, cluster_ref, order_ref, sem):
    staged((x_hbm, cluster_hbm, order_hbm), (x_ref, cluster_ref, order_ref), sem)
    cluster = cluster_ref[...].astype(jnp.float32)
    norm, _, inside = row_facts(x_ref[...], cluster, order_ref[...].astype(jnp.float32))
    out_ref[0:1, :] = norm
    out_ref[1:2, :] = cluster * float(SLOTS) + inside


def own_call(kernel, out, x, cluster, order):
    return pl.pallas_call(
        kernel,
        out_shape=out,
        in_specs=[pl.BlockSpec(memory_space=pltpu.HBM)] * 3,
        scratch_shapes=[
            pltpu.VMEM(x.shape, x.dtype),
            pltpu.VMEM((1, ROWS), jnp.int32),
            pltpu.VMEM((1, ROWS), jnp.int32),
            pltpu.SemaphoreType.DMA((3,)),
        ],
        compiler_params=pltpu.CompilerParams(vmem_limit_bytes=OWN_LIMIT * MIB),
    )(x, cluster.reshape(1, ROWS), order.reshape(1, ROWS))


def line_weights():
    line, lane = iota((16, 128), 0), iota((16, 128), 1)
    weights = jnp.zeros((16, 128), jnp.float32)
    for at, of, weight in ((0, 0, ORDERS), (0, 1, 256.0), (0, 2, 1.0), (1, 0, ORDERS)):
        weights = jnp.where((line == at) & (lane == of), weight, weights)
    return weights.astype(jnp.bfloat16)


def spread_weights():
    line, lane = iota((128, 256), 0), iota((128, 256), 1)
    weights = jnp.zeros((128, 256), jnp.float32)
    for of, weight in ((0, ORDERS), (1, 256.0), (2, 1.0)):
        weights = jnp.where((line == of) & (lane < 128), weight, weights)
    return jnp.where((line >= 3) & (line <= 5) & (lane >= 128), 1.0, weights).astype(jnp.bfloat16)


def by_lines(weights, meta):
    return lax.dot_general(weights, meta, (((1,), (1,)), ((), ())), preferred_element_type=jnp.float32)


def into_slots(rows, meta):
    wide = meta.astype(jnp.float32)
    slot = wide[0:1] * float(SLOTS) + wide[6:7]
    pick = (iota((CLUSTERS * SLOTS, ROWS), 0).astype(jnp.float32) == slot).astype(jnp.bfloat16)
    both = [jnp.dot(pick, v, preferred_element_type=jnp.float32).astype(jnp.bfloat16) for v in (rows, tall(meta))]
    return [v.reshape(CLUSTERS, SLOTS, v.shape[1]) for v in both]


def home(place_ref, offset):
    return pl.ds(pl.multiple_of(lax.rem(place_ref[0] + offset, 8) * SLOTS, SLOTS), SLOTS)


def spread_kernel(offsets, place_ref, *refs):
    slots, slot_meta = refs[-2:]
    for ref, offset in zip(refs, offsets):
        at = home(place_ref, offset)
        slots[:, at, :], slot_meta[:, at, :] = into_slots(ref[0:ROWS, :], ref[ROWS:AUG, 0:ROWS])


def spread(place, rows, offsets):
    vmem, smem = pl.BlockSpec(memory_space=pltpu.VMEM), pl.BlockSpec(memory_space=pltpu.SMEM)
    width = rows[0].shape[1]
    return pl.pallas_call(
        functools.partial(spread_kernel, offsets),
        out_shape=(
            jax.ShapeDtypeStruct((CLUSTERS, 8 * SLOTS, width), jnp.bfloat16),
            jax.ShapeDtypeStruct((CLUSTERS, 8 * SLOTS, 128), jnp.bfloat16),
        ),
        in_specs=[smem] + [vmem] * len(rows),
        out_specs=(vmem, vmem),
        compiler_params=pltpu.CompilerParams(vmem_limit_bytes=24 * MIB),
    )(place, *rows)


OWN_LIMIT = 56
MATCH_LIMIT = 52
TOP = 144
TEAM = 4


def match_kernel(
    offset, table_ref, place_ref, last_ref, slots_hbm, slot_meta_hbm, cols_hbm, out_ref,
    held, held_lanes, slots, slot_meta, slot_lines, last_slots, last_meta, waited, sem,
):
    blocks = cols_hbm.shape[0] // AUG

    def part(b, first, last, kind):
        source = cols_hbm.at[b * AUG + first : b * AUG + last, :]
        return pltpu.make_async_copy(source, held.at[b, first:last, :], sem.at[kind, b])

    def team(k):
        at = pl.ds(k * TEAM, TEAM)
        return pltpu.make_async_copy(slots_hbm.at[at], slots.at[at], sem.at[3, k])

    notes = [part(b, ROWS, AUG, 0) for b in range(blocks)]
    tops = [part(b, 0, TOP, 1) for b in range(blocks)]
    rests = [part(b, TOP, ROWS, 2) for b in range(blocks)]
    small = pltpu.make_async_copy(slot_meta_hbm, slot_meta, sem.at[4, 0])
    for copy in [*notes, small, *tops, team(0), *rests] + [team(k) for k in range(1, CLUSTERS // TEAM)]:
        copy.start()
    waited[0] = 0
    last_slots[...], last_meta[...] = into_slots(last_ref[0:ROWS, :], last_ref[ROWS:AUG, 0:ROWS])
    weights = spread_weights()
    for b, copy in enumerate(notes):
        copy.wait()
        meta = tall(held[b, ROWS:AUG, 0:ROWS])
        held_lanes[b] = jnp.dot(meta, weights, preferred_element_type=jnp.float32)
    at = home(place_ref, offset)
    small.wait()
    slot_meta[:, at, :] = last_meta[...]
    weights = line_weights()
    for g in range(CLUSTERS):
        slot_lines[g] = by_lines(weights, slot_meta[g])[0:8]
    for copy in tops:
        copy.wait()
    groups = blocks * WINDOW // 8

    def cluster(g):
        starts = [pl.multiple_of(table_ref[b, g], 16) for b in range(blocks)]
        window = jnp.concatenate([held[b, pl.ds(starts[b], WINDOW), :] for b in range(blocks)], axis=0)
        lanes = jnp.concatenate([held_lanes[b, pl.ds(starts[b], WINDOW), :] for b in range(blocks)], axis=0)
        score = by_lines(window, slots[g])
        key = lanes[:, 0:128].reshape(groups, 8, 128)
        norm = lanes[:, 128:256].reshape(groups, 8, 128)
        halves = []
        for half in (0, 128):
            row_key, row_floor = slot_lines[g, 0:1, half : half + 128], slot_lines[g, 1:2, half : half + 128]
            valid = (key < row_key) & (key >= row_floor)
            scaled = score[:, half : half + 128].reshape(groups, 8, 128) * norm
            halves.append(jnp.max(jnp.where(valid, scaled, LOW), axis=0))
        best = jnp.concatenate(halves, axis=1)
        out_ref[g] = jnp.max(best, axis=0, keepdims=True)

    def step(k, carry):
        end = functools.reduce(jnp.maximum, [table_ref[b, k * TEAM + TEAM - 1] for b in range(blocks)]) + WINDOW

        @pl.when((waited[0] == 0) & ((end > TOP) | (k == CLUSTERS // TEAM - 1)))
        def _():
            for copy in rests:
                copy.wait()
            waited[0] = 1

        team(k).wait()
        of = pl.ds(k * TEAM, TEAM)
        slots[of, at, :] = last_slots[of]
        for i in range(TEAM):
            cluster(k * TEAM + i)
        return carry

    lax.fori_loop(0, CLUSTERS // TEAM, step, 0)


def match(table, place, last, offset, slots, slot_meta, cols):
    width = cols.shape[1]
    blocks = cols.shape[0] // AUG
    vmem, smem = pl.BlockSpec(memory_space=pltpu.VMEM), pl.BlockSpec(memory_space=pltpu.SMEM)
    hbm = pl.BlockSpec(memory_space=pltpu.HBM)
    return pl.pallas_call(
        functools.partial(match_kernel, offset),
        out_shape=jax.ShapeDtypeStruct((CLUSTERS, 1, 8 * SLOTS), jnp.float32),
        in_specs=[smem, smem, vmem, hbm, hbm, hbm],
        out_specs=vmem,
        scratch_shapes=[
            pltpu.VMEM((blocks, AUG, width), jnp.bfloat16),
            pltpu.VMEM((blocks, ROWS, 256), jnp.float32),
            pltpu.VMEM((CLUSTERS, 8 * SLOTS, width), jnp.bfloat16),
            pltpu.VMEM((CLUSTERS, 8 * SLOTS, 128), jnp.bfloat16),
            pltpu.VMEM((CLUSTERS, 8, 8 * SLOTS), jnp.float32),
            pltpu.VMEM((CLUSTERS, SLOTS, width), jnp.bfloat16),
            pltpu.VMEM((CLUSTERS, SLOTS, 128), jnp.bfloat16),
            pltpu.SMEM((1,), jnp.int32),
            pltpu.SemaphoreType.DMA((5, blocks)),
        ],
        compiler_params=pltpu.CompilerParams(vmem_limit_bytes=MATCH_LIMIT * MIB),
    )(table, place, last, slots, slot_meta, cols)


def collect_kernel(found_ref, own_ref, out_ref):
    found = jnp.max(found_ref[...], axis=0, keepdims=True)
    column = jnp.concatenate([turn(found[:, h : h + 256]) for h in (0, 256)], axis=0)
    for half in (0, 128):
        part = slice(half, half + 128)
        mine = iota((CLUSTERS * SLOTS, 128), 0).astype(jnp.float32) == own_ref[1:2, part]
        best = jnp.max(jnp.where(mine, column, LOW), axis=0, keepdims=True)
        out_ref[:, part] = jnp.maximum(best * own_ref[0:1, part], -1.0)


def collect(found, own):
    return pl.pallas_call(
        collect_kernel,
        out_shape=jax.ShapeDtypeStruct((1, ROWS), jnp.float32),
    )(found, own)


def ring(size, step):
    return [(i, (i + step) % size) for i in range(size)]


def per_device(embeddings, cluster_id, member_order):
    mine = (embeddings, cluster_id, member_order)
    width = embeddings.shape[1]
    hold = lax.optimization_barrier
    own = own_call(prepare_kernel, jax.ShapeDtypeStruct((AUG, width), jnp.bfloat16), *mine)
    cols = lax.all_gather(own, "grp", axis=0, tiled=True)

    up = lambda v: lax.ppermute(v, "span", ring(8, 1))
    down = lambda v: lax.ppermute(v, "span", ring(8, -1))
    u1, d1 = up(own), down(own)
    known = own_call(remember_kernel, jax.ShapeDtypeStruct((2, ROWS), jnp.float32), *mine)
    u1, known = hold((u1, known))
    u2, d2 = up(u1), down(d1)
    u3, d3 = up(u2), down(d2)
    u4 = up(u3)
    place = lax.axis_index("span").astype(jnp.int32).reshape(1)
    slots, slot_meta = spread(place, [own, u1, d1, u2, d2, u3, d3], (0, 7, 1, 6, 2, 5, 3))

    tables = cols.reshape(16, AUG, width)[:, ROWS + START, 0:CLUSTERS].astype(jnp.int32)
    found = match(tables, place, u4, 4, slots, slot_meta, cols).reshape(CLUSTERS, 8, SLOTS)
    found = found.transpose(1, 0, 2).reshape(8, CLUSTERS * SLOTS)
    arrived = lax.all_to_all(found, "span", split_axis=0, concat_axis=0, tiled=True)
    return collect(arrived, known)[0]


def solution(mesh):
    return jax.shard_map(
        per_device,
        mesh=mesh,
        in_specs=(
            P(("outer", "grp", "span"), None),
            P(("outer", "grp", "span")),
            P(("outer", "grp", "span")),
        ),
        out_specs=P(("outer", "grp", "span")),
        check_vma=False,
    )
```

time: 122 us -> 116 us (0.951)
  waiting for transfers between devices: 43.3 us -> 31.7 us
  Pallas kernels: 21.4 us -> 24.7 us
  local copies, waits for them, and re-layouts: 5.14 us -> 7.72 us
    all_gather x1, waiting for transfers between devices: 13.5 us -> 4.54 us  [per_device(): cols = lax.all_gather(own, 'grp', axis=0, tiled=True)]
    pallas_call x2 -> x4, Pallas kernels: 20 us -> 23.3 us  [the longest x1 15.1 us: match(): pl.pallas_call(functools.partial(match_kernel, offset), out_shape=jax.Sha...]
    ppermute x4, waiting for transfers between devices: 29.8 us -> 27.1 us  [per_device(): up = lambda v: lax.ppermute(v, 'span', ring(8, 1))]
    unnamed x11 -> x9, local copies, waits for them, and re-layouts: 4.18 us -> 6.77 us
  transfers between devices with their start and end apart: 8 -> 8, of which waited for: 4 -> 4; matrix products, arithmetic and copies ran while one was open for 1% -> 1% of each run, Pallas kernels for 0% -> 5%
where the time goes in v3:
time: 116 us; the launch traced here: 115 us
  waiting for transfers between devices  31.7 us (27%)
  Pallas kernels  24.7 us (21%)
  starting transfers between devices  23.3 us (20%)
  blocking collectives  14.3 us (12%)
  between operations  13.6 us (12%)
  local copies, waits for them, and re-layouts  7.72 us (7%)
    ppermute x4, waiting for transfers between devices, per_device(): up = lambda v: lax.ppermute(v, 'span', ring(8, 1))  27.1 us
    pallas_call x1, Pallas kernels, match(): pl.pallas_call(functools.partial(match_kernel, offset), out_shape=jax.Sha...  15.1 us
    all_to_all x1, blocking collectives, per_device(): lax.all_to_all(found, 'span', split_axis=0, concat_axis=0, tiled=True)  14.3 us
    ppermute x3, starting transfers between devices, per_device(): down = lambda v: lax.ppermute(v, 'span', ring(8, -1))  14.1 us
    ppermute x4, starting transfers between devices, per_device(): up = lambda v: lax.ppermute(v, 'span', ring(8, 1))  9.21 us
    unnamed x9, local copies, waits for them, and re-layouts  6.77 us
    all_gather x1, waiting for transfers between devices, per_device(): cols = lax.all_gather(own, 'grp', axis=0, tiled=True)  4.54 us
    pallas_call x2, Pallas kernels, own_call(): pl.pallas_call(kernel, out_shape=out, in_specs=[pl.BlockSpec(memory_space...  4.32 us
  transfers between devices with their start and end apart: 8, of which 4 were waited for; matrix products, arithmetic and copies ran while one was open for 1% of the time, Pallas kernels for 5%

profile of v3, /device:TPU:2, one launch (start us, length us, event | category | flops | bytes accessed | tf_op | source)
XLA Modules:
  0.0 115.3 jit_solution(16066010314834281525)
XLA Ops:
  6.5 2.4 %shard_map.37.refs_0_ = bf16[272,1024]{1,0:T(8,128)(2,1)} custom-call(bf16[256,1024]{1,0:T(8,128)(2,1)} %x_hbm.3, s32[1,256]{1,0:T(1,128)} %bitcast.17, s32[1,256]{1,0:T(1,128)} %bitcast.19), custom_call_target="tpu_custom_call" | custom-call | tf_op jit(solution)/shard_map/pallas_call | solution.py:91
  8.9 0.0 all-gather.2.cloned.1.call-update
  9.0 3.5 %collective-permute-start = (bf16[272,1024]{1,0:T(8,128)(2,1)}, bf16[272,1024]{1,0:T(8,128)(2,1)S(1)}, u32[]{:S(2)}, u32[]{:S(2)}) collective-permute-start(bf16[272,1024]{1,0:T(8,128)(2,1)} %shard_map.37.refs_0_), channel_id=1, source_target_pairs={{0,1},{1,2},{2,3},{3,4},{4,5},{5,6},{6,7},{7,0},{8,9},{9,10},{10,1... | collective-permute-start | bytes 1671176 | tf_op jit(solution)/shard_map/ppermute | solution.py:290
  12.4 3.8 %collective-permute-start.4 = (bf16[272,1024]{1,0:T(8,128)(2,1)}, bf16[272,1024]{1,0:T(8,128)(2,1)S(1)}, u32[]{:S(2)}, u32[]{:S(2)}) collective-permute-start(bf16[272,1024]{1,0:T(8,128)(2,1)} %shard_map.37.refs_0_), channel_id=1, source_target_pairs={{0,7},{1,0},{2,1},{3,2},{4,3},{5,4},{6,5},{7,6},{8,15},{9,8},{10,9... | collective-permute-start | bytes 1671176 | tf_op jit(solution)/shard_map/ppermute | solution.py:291
  16.3 1.9 %shard_map.38.own_ref = f32[2,256]{1,0:T(2,128)} custom-call(bf16[256,1024]{1,0:T(8,128)(2,1)} %x_hbm.3, s32[1,256]{1,0:T(1,128)} %bitcast.18, s32[1,256]{1,0:T(1,128)} %bitcast.20), custom_call_target="tpu_custom_call" | custom-call | tf_op jit(solution)/shard_map/pallas_call | solution.py:91
  18.2 8.9 %collective-permute-done.refs_1_ = bf16[272,1024]{1,0:T(8,128)(2,1)S(1)} collective-permute-done((bf16[272,1024]{1,0:T(8,128)(2,1)}, bf16[272,1024]{1,0:T(8,128)(2,1)S(1)}, u32[]{:S(2)}, u32[]{:S(2)}) %collective-permute-start) | collective-permute-done | bytes 557088 | tf_op jit(solution)/shard_map/ppermute | solution.py:290
  27.2 1.9 %collective-permute-start.1 = (bf16[272,1024]{1,0:T(8,128)(2,1)S(1)}, bf16[272,1024]{1,0:T(8,128)(2,1)S(1)}, u32[]{:S(2)}, u32[]{:S(2)}) collective-permute-start(bf16[272,1024]{1,0:T(8,128)(2,1)S(1)} %collective-permute-done.refs_1_), channel_id=1, source_target_pairs={{0,1},{1,2},{2,3},{3,4},{4,5},{5,6},{6,7},{7,0},{8,9},{9,10},{10,1... | collective-permute-start | bytes 1671176 | tf_op jit(solution)/shard_map/ppermute | solution.py:290
  29.1 0.0 collective-permute-done.4.refs_2_
  29.1 5.1 %collective-permute-start.5 = (bf16[272,1024]{1,0:T(8,128)(2,1)S(1)}, bf16[272,1024]{1,0:T(8,128)(2,1)S(1)}, u32[]{:S(2)}, u32[]{:S(2)}) collective-permute-start(bf16[272,1024]{1,0:T(8,128)(2,1)S(1)} %collective-permute-done.4.refs_2_), channel_id=1, source_target_pairs={{0,7},{1,0},{2,1},{3,2},{4,3},{5,4},{6,5},{7,6},{8,15},{9,8},{10,9... | collective-permute-start | bytes 1671176 | tf_op jit(solution)/shard_map/ppermute | solution.py:291
  34.2 9.8 %collective-permute-done.1.refs_3_ = bf16[272,1024]{1,0:T(8,128)(2,1)S(1)} collective-permute-done((bf16[272,1024]{1,0:T(8,128)(2,1)S(1)}, bf16[272,1024]{1,0:T(8,128)(2,1)S(1)}, u32[]{:S(2)}, u32[]{:S(2)}) %collective-permute-start.1) | collective-permute-done | bytes 557088 | tf_op jit(solution)/shard_map/ppermute | solution.py:290
  44.1 1.9 %collective-permute-start.2 = (bf16[272,1024]{1,0:T(8,128)(2,1)S(1)}, bf16[272,1024]{1,0:T(8,128)(2,1)}, u32[]{:S(2)}, u32[]{:S(2)}) collective-permute-start(bf16[272,1024]{1,0:T(8,128)(2,1)S(1)} %collective-permute-done.1.refs_3_), channel_id=1, source_target_pairs={{0,1},{1,2},{2,3},{3,4},{4,5},{5,6},{6,7},{7,0},{8,9},{9,10},{10,1... | collective-permute-start | bytes 1671176 | tf_op jit(solution)/shard_map/ppermute | solution.py:290
  46.0 0.0 collective-permute-done.5.refs_4_
  46.0 5.1 %collective-permute-start.6 = (bf16[272,1024]{1,0:T(8,128)(2,1)S(1)}, bf16[272,1024]{1,0:T(8,128)(2,1)}, u32[]{:S(2)}, u32[]{:S(2)}) collective-permute-start(bf16[272,1024]{1,0:T(8,128)(2,1)S(1)} %collective-permute-done.5.refs_4_), channel_id=1, source_target_pairs={{0,7},{1,0},{2,1},{3,2},{4,3},{5,4},{6,5},{7,6},{8,15},{9,8},{10,9... | collective-permute-start | bytes 1671176 | tf_op jit(solution)/shard_map/ppermute | solution.py:291
  51.1 0.8 copy-done.2
  52.0 8.3 %collective-permute-done.2.refs_5_ = bf16[272,1024]{1,0:T(8,128)(2,1)} collective-permute-done((bf16[272,1024]{1,0:T(8,128)(2,1)S(1)}, bf16[272,1024]{1,0:T(8,128)(2,1)}, u32[]{:S(2)}, u32[]{:S(2)}) %collective-permute-start.2) | collective-permute-done | bytes 557088 | tf_op jit(solution)/shard_map/ppermute | solution.py:290
  60.3 1.9 %collective-permute-start.3 = (bf16[272,1024]{1,0:T(8,128)(2,1)}, bf16[272,1024]{1,0:T(8,128)(2,1)S(1)}, u32[]{:S(2)}, u32[]{:S(2)}) collective-permute-start(bf16[272,1024]{1,0:T(8,128)(2,1)} %collective-permute-done.2.refs_5_), channel_id=1, source_target_pairs={{0,1},{1,2},{2,3},{3,4},{4,5},{5,6},{6,7},{7,0},{8,9},{9,10},{10,1... | collective-permute-start | bytes 1671176 | tf_op jit(solution)/shard_map/ppermute | solution.py:290
  62.2 0.0 collective-permute-done.6.refs_6_
  62.2 0.0 copy-start.1
  62.2 1.0 copy-done.1
  63.3 1.1 copy-done.3
  64.3 3.8 %shard_map.39 = (bf16[16,256,1024]{2,1,0:T(8,128)(2,1)S(1)}, bf16[16,256,128]{2,1,0:T(8,128)(2,1)S(1)}) custom-call(s32[1]{0:T(128)} %bitcast.4.place_ref, bf16[272,1024]{1,0:T(8,128)(2,1)S(1)} %copy-done.1, bf16[272,1024]{1,0:T(8,128)(2,1)S(1)} %collective-permute-done.refs_1_, bf16[272,1024]{1,0:T(8,128)(2,1)S(1)} %collective-permute-done.4.refs_2_, ...), custom_call_target="tpu_custom_call" | custom-call | tf_op jit(solution)/shard_map/pallas_call | solution.py:147
  68.2 0.0 copy-start
  68.2 3.2 %copy-done = bf16[16,256,1024]{2,1,0:T(8,128)(2,1)} copy-done((bf16[16,256,1024]{2,1,0:T(8,128)(2,1)}, bf16[16,256,1024]{2,1,0:T(8,128)(2,1)S(1)}, u32[]{:S(2)}) %copy-start) | copy-done | bytes 8388632
  71.4 4.5 %all-gather.2.cloned.1.call-done.cols_hbm = bf16[4352,1024]{1,0:T(8,128)(2,1)} async-done(((bf16[272,1024]{1,0:T(8,128)(2,1)}), bf16[4352,1024]{1,0:T(8,128)(2,1)}) %all-gather.2.cloned.1.call-update) | async-done | bytes 8912912 | tf_op jit(solution)/shard_map/all_gather | solution.py:288
  76.0 0.8 slice.4
  76.7 0.0 collective-permute-done.3.last_ref
  76.8 15.1 %shard_map.40 = f32[16,1,256]{2,1,0:T(1,128)S(1)} custom-call(s32[16,16]{1,0:T(8,128)S(1)} %fusion.table_ref, s32[1]{0:T(128)} %bitcast.4.place_ref, bf16[272,1024]{1,0:T(8,128)(2,1)S(1)} %collective-permute-done.3.last_ref, bf16[16,256,1024]{2,1,0:T(8,128)(2,1)} %copy-done, bf16[16,256,128]{2,1,0:T(8,128)(2,1)S(1)} %get-tuple-element.11.slot_meta_hbm, ...), custom_call_target="tpu_custom_call" | custom-call | tf_op jit(solution)/shard_map/pallas_call | solution.py:242
  91.9 0.1 reshape.27
  92.0 0.1 all_to_all.7
  92.1 14.3 %all_to_all.11 = f32[8,1,512]{2,1,0:T(1,128)S(1)} all-to-all(f32[8,1,512]{2,1,0:T(1,128)S(1)} %all_to_all.7), channel_id=1, replica_groups=mesh['outer'=4,'grp'=16,'span'=8] {'span'}, dimensions={0} | all-to-all | bytes 32768 | tf_op jit(solution)/shard_map/all_to_all | solution.py:304
  106.5 0.6 copy.14
  107.0 1.4 %shard_map.41 = f32[1,256]{1,0:T(1,128)} custom-call(f32[8,512]{1,0:T(8,128)} %bitcast.16, f32[2,256]{1,0:T(2,128)} %shard_map.38.own_ref), custom_call_target="tpu_custom_call" | custom-call | tf_op jit(solution)/shard_map/pallas_call | solution.py:273
  (6 shorter events, 0.1 us)
Async XLA Ops:
  6.5 69.4 %all-gather.2.cloned.1.call-start = ((), (), s32[]{:S(2)}) async-start(), calls=%async_computation.1 | async-start | bytes 9469952 | tf_op jit(solution)/shard_map/all_gather | solution.py:288
  9.0 18.2 %collective-permute-start = (bf16[272,1024]{1,0:T(8,128)(2,1)}, bf16[272,1024]{1,0:T(8,128)(2,1)S(1)}, u32[]{:S(2)}, u32[]{:S(2)}) collective-permute-start(bf16[272,1024]{1,0:T(8,128)(2,1)} %shard_map.37.refs_0_), channel_id=1, source_target_pairs={{0,1},{1,2},{2,3},{3,4},{4,5},{5,6},{6,7},{7,0},{8,9},{9,10},{10,1... | collective-permute-start | bytes 1671176 | tf_op jit(solution)/shard_map/ppermute | solution.py:290
  12.4 16.6 %collective-permute-start.4 = (bf16[272,1024]{1,0:T(8,128)(2,1)}, bf16[272,1024]{1,0:T(8,128)(2,1)S(1)}, u32[]{:S(2)}, u32[]{:S(2)}) collective-permute-start(bf16[272,1024]{1,0:T(8,128)(2,1)} %shard_map.37.refs_0_), channel_id=1, source_target_pairs={{0,7},{1,0},{2,1},{3,2},{4,3},{5,4},{6,5},{7,6},{8,15},{9,8},{10,9... | collective-permute-start | bytes 1671176 | tf_op jit(solution)/shard_map/ppermute | solution.py:291
  27.2 16.9 %collective-permute-start.1 = (bf16[272,1024]{1,0:T(8,128)(2,1)S(1)}, bf16[272,1024]{1,0:T(8,128)(2,1)S(1)}, u32[]{:S(2)}, u32[]{:S(2)}) collective-permute-start(bf16[272,1024]{1,0:T(8,128)(2,1)S(1)} %collective-permute-done.refs_1_), channel_id=1, source_target_pairs={{0,1},{1,2},{2,3},{3,4},{4,5},{5,6},{6,7},{7,0},{8,9},{9,10},{10,1... | collective-permute-start | bytes 1671176 | tf_op jit(solution)/shard_map/ppermute | solution.py:290
  29.1 16.9 %collective-permute-start.5 = (bf16[272,1024]{1,0:T(8,128)(2,1)S(1)}, bf16[272,1024]{1,0:T(8,128)(2,1)S(1)}, u32[]{:S(2)}, u32[]{:S(2)}) collective-permute-start(bf16[272,1024]{1,0:T(8,128)(2,1)S(1)} %collective-permute-done.4.refs_2_), channel_id=1, source_target_pairs={{0,7},{1,0},{2,1},{3,2},{4,3},{5,4},{6,5},{7,6},{8,15},{9,8},{10,9... | collective-permute-start | bytes 1671176 | tf_op jit(solution)/shard_map/ppermute | solution.py:291
  44.1 16.2 %collective-permute-start.2 = (bf16[272,1024]{1,0:T(8,128)(2,1)S(1)}, bf16[272,1024]{1,0:T(8,128)(2,1)}, u32[]{:S(2)}, u32[]{:S(2)}) collective-permute-start(bf16[272,1024]{1,0:T(8,128)(2,1)S(1)} %collective-permute-done.1.refs_3_), channel_id=1, source_target_pairs={{0,1},{1,2},{2,3},{3,4},{4,5},{5,6},{6,7},{7,0},{8,9},{9,10},{10,1... | collective-permute-start | bytes 1671176 | tf_op jit(solution)/shard_map/ppermute | solution.py:290
  46.0 16.2 %collective-permute-start.6 = (bf16[272,1024]{1,0:T(8,128)(2,1)S(1)}, bf16[272,1024]{1,0:T(8,128)(2,1)}, u32[]{:S(2)}, u32[]{:S(2)}) collective-permute-start(bf16[272,1024]{1,0:T(8,128)(2,1)S(1)} %collective-permute-done.5.refs_4_), channel_id=1, source_target_pairs={{0,7},{1,0},{2,1},{3,2},{4,3},{5,4},{6,5},{7,6},{8,15},{9,8},{10,9... | collective-permute-start | bytes 1671176 | tf_op jit(solution)/shard_map/ppermute | solution.py:291
  51.1 0.8 copy-start.2
  60.3 16.5 %collective-permute-start.3 = (bf16[272,1024]{1,0:T(8,128)(2,1)}, bf16[272,1024]{1,0:T(8,128)(2,1)S(1)}, u32[]{:S(2)}, u32[]{:S(2)}) collective-permute-start(bf16[272,1024]{1,0:T(8,128)(2,1)} %collective-permute-done.2.refs_5_), channel_id=1, source_target_pairs={{0,1},{1,2},{2,3},{3,4},{4,5},{5,6},{6,7},{7,0},{8,9},{9,10},{10,1... | collective-permute-start | bytes 1671176 | tf_op jit(solution)/shard_map/ppermute | solution.py:290
  62.2 1.1 copy-start.1
  63.3 1.1 copy-start.3
  68.2 3.3 %copy-start = (bf16[16,256,1024]{2,1,0:T(8,128)(2,1)}, bf16[16,256,1024]{2,1,0:T(8,128)(2,1)S(1)}, u32[]{:S(2)}) copy-start(bf16[16,256,1024]{2,1,0:T(8,128)(2,1)S(1)} %get-tuple-element.10.slots_hbm) | copy-start | bytes 25165828
Sparse Core Ops, SparseCore 0:
  9.5 66.4 all-gather.1

commit v4 on v3

--- a/solution.py
+++ b/solution.py
@@ -5,6 +5,7 @@
 from jax import lax
 from jax.experimental import pallas as pl
 from jax.experimental.pallas import tpu as pltpu
+from jax.sharding import Mesh
 from jax.sharding import PartitionSpec as P
 
 ROWS = 256
@@ -13,6 +14,7 @@
 WINDOW = 48
 ORDERS = 32768.0
 LOW = -1e30
+HIGH = 1e9
 MIB = 1024 * 1024
 META = 16
 AUG = ROWS + META
@@ -105,7 +107,7 @@
 def line_weights():
     line, lane = iota((16, 128), 0), iota((16, 128), 1)
     weights = jnp.zeros((16, 128), jnp.float32)
-    for at, of, weight in ((0, 0, ORDERS), (0, 1, 256.0), (0, 2, 1.0), (1, 0, ORDERS)):
+    for at, of, weight in ((0, 0, ORDERS), (0, 1, 256.0), (0, 2, 1.0)):
         weights = jnp.where((line == at) & (lane == of), weight, weights)
     return weights.astype(jnp.bfloat16)
 
@@ -163,8 +165,8 @@
 
 
 def match_kernel(
-    offset, table_ref, place_ref, last_ref, slots_hbm, slot_meta_hbm, cols_hbm, out_ref,
-    held, held_lanes, slots, slot_meta, slot_lines, last_slots, last_meta, waited, sem,
+    offset, place_ref, last_ref, slots_hbm, slot_meta_hbm, cols_hbm, out_ref,
+    held, held_lanes, slots, slot_meta, slot_lines, last_slots, last_meta, starts_vmem, table_ref, waited, sem,
 ):
     blocks = cols_hbm.shape[0] // AUG
 
@@ -180,23 +182,32 @@
     tops = [part(b, 0, TOP, 1) for b in range(blocks)]
     rests = [part(b, TOP, ROWS, 2) for b in range(blocks)]
     small = pltpu.make_async_copy(slot_meta_hbm, slot_meta, sem.at[4, 0])
-    for copy in [*notes, small, *tops, team(0), *rests] + [team(k) for k in range(1, CLUSTERS // TEAM)]:
+    for copy in [*notes, small]:
         copy.start()
     waited[0] = 0
     last_slots[...], last_meta[...] = into_slots(last_ref[0:ROWS, :], last_ref[ROWS:AUG, 0:ROWS])
     weights = spread_weights()
-    for b, copy in enumerate(notes):
+    for copy in notes:
         copy.wait()
+    for copy in [*tops, team(0)]:
+        copy.start()
+    for b in range(blocks):
         meta = tall(held[b, ROWS:AUG, 0:ROWS])
         held_lanes[b] = jnp.dot(meta, weights, preferred_element_type=jnp.float32)
+        starts_vmem[b : b + 1, :] = held[b, ROWS:AUG, 0:128].astype(jnp.float32)[START : START + 1].astype(jnp.int32)
+    table = pltpu.make_async_copy(starts_vmem, table_ref, sem.at[4, 1])
+    table.start()
     at = home(place_ref, offset)
     small.wait()
     slot_meta[:, at, :] = last_meta[...]
     weights = line_weights()
     for g in range(CLUSTERS):
         slot_lines[g] = by_lines(weights, slot_meta[g])[0:8]
+    table.wait()
     for copy in tops:
         copy.wait()
+    for copy in rests:
+        copy.start()
     groups = blocks * WINDOW // 8
 
     def cluster(g):
@@ -204,18 +215,22 @@
         window = jnp.concatenate([held[b, pl.ds(starts[b], WINDOW), :] for b in range(blocks)], axis=0)
         lanes = jnp.concatenate([held_lanes[b, pl.ds(starts[b], WINDOW), :] for b in range(blocks)], axis=0)
         score = by_lines(window, slots[g])
-        key = lanes[:, 0:128].reshape(groups, 8, 128)
+        key = lanes[:, 0:128]
+        key = jnp.where(key >= (g * int(ORDERS)).astype(jnp.float32), key, HIGH).reshape(groups, 8, 128)
         norm = lanes[:, 128:256].reshape(groups, 8, 128)
         halves = []
         for half in (0, 128):
-            row_key, row_floor = slot_lines[g, 0:1, half : half + 128], slot_lines[g, 1:2, half : half + 128]
-            valid = (key < row_key) & (key >= row_floor)
+            valid = key < slot_lines[g, 0:1, half : half + 128]
             scaled = score[:, half : half + 128].reshape(groups, 8, 128) * norm
             halves.append(jnp.max(jnp.where(valid, scaled, LOW), axis=0))
         best = jnp.concatenate(halves, axis=1)
         out_ref[g] = jnp.max(best, axis=0, keepdims=True)
 
     def step(k, carry):
+        @pl.when(k + 1 < CLUSTERS // TEAM)
+        def _():
+            team(k + 1).start()
+
         end = functools.reduce(jnp.maximum, [table_ref[b, k * TEAM + TEAM - 1] for b in range(blocks)]) + WINDOW
 
         @pl.when((waited[0] == 0) & ((end > TOP) | (k == CLUSTERS // TEAM - 1)))
@@ -234,7 +249,7 @@
     lax.fori_loop(0, CLUSTERS // TEAM, step, 0)
 
 
-def match(table, place, last, offset, slots, slot_meta, cols):
+def match(place, last, offset, slots, slot_meta, cols):
     width = cols.shape[1]
     blocks = cols.shape[0] // AUG
     vmem, smem = pl.BlockSpec(memory_space=pltpu.VMEM), pl.BlockSpec(memory_space=pltpu.SMEM)
@@ -242,7 +257,7 @@
     return pl.pallas_call(
         functools.partial(match_kernel, offset),
         out_shape=jax.ShapeDtypeStruct((CLUSTERS, 1, 8 * SLOTS), jnp.float32),
-        in_specs=[smem, smem, vmem, hbm, hbm, hbm],
+        in_specs=[smem, vmem, hbm, hbm, hbm],
         out_specs=vmem,
         scratch_shapes=[
             pltpu.VMEM((blocks, AUG, width), jnp.bfloat16),
@@ -252,15 +267,17 @@
             pltpu.VMEM((CLUSTERS, 8, 8 * SLOTS), jnp.float32),
             pltpu.VMEM((CLUSTERS, SLOTS, width), jnp.bfloat16),
             pltpu.VMEM((CLUSTERS, SLOTS, 128), jnp.bfloat16),
+            pltpu.VMEM((blocks, 128), jnp.int32),
+            pltpu.SMEM((blocks, 128), jnp.int32),
             pltpu.SMEM((1,), jnp.int32),
             pltpu.SemaphoreType.DMA((5, blocks)),
         ],
         compiler_params=pltpu.CompilerParams(vmem_limit_bytes=MATCH_LIMIT * MIB),
-    )(table, place, last, slots, slot_meta, cols)
+    )(place, last, slots, slot_meta, cols)
 
 
 def collect_kernel(found_ref, own_ref, out_ref):
-    found = jnp.max(found_ref[...], axis=0, keepdims=True)
+    found = jnp.max(found_ref[...], axis=0)
     column = jnp.concatenate([turn(found[:, h : h + 256]) for h in (0, 256)], axis=0)
     for half in (0, 128):
         part = slice(half, half + 128)
@@ -285,35 +302,32 @@
     width = embeddings.shape[1]
     hold = lax.optimization_barrier
     own = own_call(prepare_kernel, jax.ShapeDtypeStruct((AUG, width), jnp.bfloat16), *mine)
-    cols = lax.all_gather(own, "grp", axis=0, tiled=True)
-
-    up = lambda v: lax.ppermute(v, "span", ring(8, 1))
-    down = lambda v: lax.ppermute(v, "span", ring(8, -1))
+    cols = lax.all_gather(own, ("z", "core"), axis=0, tiled=True)
+
+    up = lambda v: lax.ppermute(v, "y", ring(8, 1))
+    down = lambda v: lax.ppermute(v, "y", ring(8, -1))
     u1, d1 = up(own), down(own)
     known = own_call(remember_kernel, jax.ShapeDtypeStruct((2, ROWS), jnp.float32), *mine)
     u1, known = hold((u1, known))
     u2, d2 = up(u1), down(d1)
     u3, d3 = up(u2), down(d2)
     u4 = up(u3)
-    place = lax.axis_index("span").astype(jnp.int32).reshape(1)
+    place = lax.axis_index("y").astype(jnp.int32).reshape(1)
     slots, slot_meta = spread(place, [own, u1, d1, u2, d2, u3, d3], (0, 7, 1, 6, 2, 5, 3))
 
-    tables = cols.reshape(16, AUG, width)[:, ROWS + START, 0:CLUSTERS].astype(jnp.int32)
-    found = match(tables, place, u4, 4, slots, slot_meta, cols).reshape(CLUSTERS, 8, SLOTS)
-    found = found.transpose(1, 0, 2).reshape(8, CLUSTERS * SLOTS)
-    arrived = lax.all_to_all(found, "span", split_axis=0, concat_axis=0, tiled=True)
+    found = match(place, u4, 4, slots, slot_meta, cols).reshape(CLUSTERS, 8, SLOTS)
+    found = found.transpose(1, 0, 2).reshape(8, 1, CLUSTERS * SLOTS)
+    arrived = lax.all_to_all(found, "y", split_axis=0, concat_axis=0, tiled=True)
     return collect(arrived, known)[0]
 
 
 def solution(mesh):
+    axes = ("x", "z", "core", "y")
+    finer = Mesh(mesh.devices.reshape(mesh.shape["outer"], 8, 2, 8), axes)
     return jax.shard_map(
         per_device,
-        mesh=mesh,
-        in_specs=(
-            P(("outer", "grp", "span"), None),
-            P(("outer", "grp", "span")),
-            P(("outer", "grp", "span")),
-        ),
-        out_specs=P(("outer", "grp", "span")),
+        mesh=finer,
+        in_specs=(P(axes, None), P(axes), P(axes)),
+        out_specs=P(axes),
         check_vma=False,
     )

time: 116 us -> 112 us (0.966)
  Pallas kernels: 24.7 us -> 22.5 us
  local copies, waits for them, and re-layouts: 7.72 us -> 6.36 us
    all_gather x1, waiting for transfers between devices: 4.54 us -> 0.32 us  [per_device(): cols = lax.all_gather(own, ('z', 'core'), axis=0, tiled=True)]
    ppermute x7, waiting for transfers between devices: 27.1 us -> 31.3 us  [the longest x4 31.3 us: per_device(): up = lambda v: lax.ppermute(v, 'y', ring(8, 1))]
    pallas_call x1, Pallas kernels: 15.1 us -> 12.9 us  [match(): pl.pallas_call(functools.partial(match_kernel, offset), out_shape=jax.Sha...]
    unnamed x9 -> x8, local copies, waits for them, and re-layouts: 6.77 us -> 6.17 us
  transfers between devices with their start and end apart: 8 -> 8, of which waited for: 4 -> 5; matrix products, arithmetic and copies ran while one was open for 1% -> 0% of each run, Pallas kernels for 5% -> 5%
where the time goes in v4:
time: 112 us
  waiting for transfers between devices  31.7 us (28%)
  starting transfers between devices  23.3 us (21%)
  Pallas kernels  22.5 us (20%)
  blocking collectives  14.4 us (13%)
  between operations  13.6 us (12%)
  local copies, waits for them, and re-layouts  6.36 us (6%)
    ppermute x4, waiting for transfers between devices, per_device(): up = lambda v: lax.ppermute(v, 'y', ring(8, 1))  31.3 us
    all_to_all x1, blocking collectives, per_device(): lax.all_to_all(found, 'y', split_axis=0, concat_axis=0, tiled=True)  14.4 us
    ppermute x3, starting transfers between devices, per_device(): down = lambda v: lax.ppermute(v, 'y', ring(8, -1))  14.1 us
    pallas_call x1, Pallas kernels, match(): pl.pallas_call(functools.partial(match_kernel, offset), out_shape=jax.Sha...  12.9 us
    ppermute x4, starting transfers between devices, per_device(): up = lambda v: lax.ppermute(v, 'y', ring(8, 1))  9.21 us
    unnamed x8, local copies, waits for them, and re-layouts  6.17 us
    pallas_call x2, Pallas kernels, own_call(): pl.pallas_call(kernel, out_shape=out, in_specs=[pl.BlockSpec(memory_space...  4.32 us
    pallas_call x1, Pallas kernels, spread(): pl.pallas_call(functools.partial(spread_kernel, offsets), out_shape=(jax....  3.84 us
  transfers between devices with their start and end apart: 8, of which 5 were waited for; matrix products, arithmetic and copies ran while one was open for 0% of the time, Pallas kernels for 5%

profile of v4, /device:TPU:2, one launch (start us, length us, event | category | flops | bytes accessed | tf_op | source)
XLA Modules:
  0.0 111.8 jit_solution(3041920822742951580)
XLA Ops:
  6.5 0.0 all-gather.2.cloned.1.call-start
  6.5 2.4 %shard_map.37.refs_0_ = bf16[272,1024]{1,0:T(8,128)(2,1)} custom-call(bf16[256,1024]{1,0:T(8,128)(2,1)} %x_hbm.3, s32[1,256]{1,0:T(1,128)} %bitcast.8, s32[1,256]{1,0:T(1,128)} %bitcast.10), custom_call_target="tpu_custom_call" | custom-call | tf_op jit(solution)/shard_map/pallas_call | solution.py:93
  8.9 0.0 all-gather.2.cloned.1.call-update
  9.0 3.5 %collective-permute-start = (bf16[272,1024]{1,0:T(8,128)(2,1)}, bf16[272,1024]{1,0:T(8,128)(2,1)S(1)}, u32[]{:S(2)}, u32[]{:S(2)}) collective-permute-start(bf16[272,1024]{1,0:T(8,128)(2,1)} %shard_map.37.refs_0_), channel_id=1, source_target_pairs={{0,1},{1,2},{2,3},{3,4},{4,5},{5,6},{6,7},{7,0},{8,9},{9,10},{10,1... | collective-permute-start | bytes 1671176 | tf_op jit(solution)/shard_map/ppermute | solution.py:307
  12.4 3.8 %collective-permute-start.4 = (bf16[272,1024]{1,0:T(8,128)(2,1)}, bf16[272,1024]{1,0:T(8,128)(2,1)S(1)}, u32[]{:S(2)}, u32[]{:S(2)}) collective-permute-start(bf16[272,1024]{1,0:T(8,128)(2,1)} %shard_map.37.refs_0_), channel_id=1, source_target_pairs={{0,7},{1,0},{2,1},{3,2},{4,3},{5,4},{6,5},{7,6},{8,15},{9,8},{10,9... | collective-permute-start | bytes 1671176 | tf_op jit(solution)/shard_map/ppermute | solution.py:308
  16.3 1.9 %shard_map.38.own_ref = f32[2,256]{1,0:T(2,128)} custom-call(bf16[256,1024]{1,0:T(8,128)(2,1)} %x_hbm.3, s32[1,256]{1,0:T(1,128)} %bitcast.9, s32[1,256]{1,0:T(1,128)} %bitcast.11), custom_call_target="tpu_custom_call" | custom-call | tf_op jit(solution)/shard_map/pallas_call | solution.py:93
  18.2 8.9 %collective-permute-done.refs_1_ = bf16[272,1024]{1,0:T(8,128)(2,1)S(1)} collective-permute-done((bf16[272,1024]{1,0:T(8,128)(2,1)}, bf16[272,1024]{1,0:T(8,128)(2,1)S(1)}, u32[]{:S(2)}, u32[]{:S(2)}) %collective-permute-start) | collective-permute-done | bytes 557088 | tf_op jit(solution)/shard_map/ppermute | solution.py:307
  27.2 1.9 %collective-permute-start.1 = (bf16[272,1024]{1,0:T(8,128)(2,1)S(1)}, bf16[272,1024]{1,0:T(8,128)(2,1)S(1)}, u32[]{:S(2)}, u32[]{:S(2)}) collective-permute-start(bf16[272,1024]{1,0:T(8,128)(2,1)S(1)} %collective-permute-done.refs_1_), channel_id=1, source_target_pairs={{0,1},{1,2},{2,3},{3,4},{4,5},{5,6},{6,7},{7,0},{8,9},{9,10},{10,1... | collective-permute-start | bytes 1671176 | tf_op jit(solution)/shard_map/ppermute | solution.py:307
  29.1 0.0 collective-permute-done.4.refs_2_
  29.1 5.1 %collective-permute-start.5 = (bf16[272,1024]{1,0:T(8,128)(2,1)S(1)}, bf16[272,1024]{1,0:T(8,128)(2,1)S(1)}, u32[]{:S(2)}, u32[]{:S(2)}) collective-permute-start(bf16[272,1024]{1,0:T(8,128)(2,1)S(1)} %collective-permute-done.4.refs_2_), channel_id=1, source_target_pairs={{0,7},{1,0},{2,1},{3,2},{4,3},{5,4},{6,5},{7,6},{8,15},{9,8},{10,9... | collective-permute-start | bytes 1671176 | tf_op jit(solution)/shard_map/ppermute | solution.py:308
  34.2 9.8 %collective-permute-done.1.refs_3_ = bf16[272,1024]{1,0:T(8,128)(2,1)S(1)} collective-permute-done((bf16[272,1024]{1,0:T(8,128)(2,1)S(1)}, bf16[272,1024]{1,0:T(8,128)(2,1)S(1)}, u32[]{:S(2)}, u32[]{:S(2)}) %collective-permute-start.1) | collective-permute-done | bytes 557088 | tf_op jit(solution)/shard_map/ppermute | solution.py:307
  44.1 1.9 %collective-permute-start.2 = (bf16[272,1024]{1,0:T(8,128)(2,1)S(1)}, bf16[272,1024]{1,0:T(8,128)(2,1)}, u32[]{:S(2)}, u32[]{:S(2)}) collective-permute-start(bf16[272,1024]{1,0:T(8,128)(2,1)S(1)} %collective-permute-done.1.refs_3_), channel_id=1, source_target_pairs={{0,1},{1,2},{2,3},{3,4},{4,5},{5,6},{6,7},{7,0},{8,9},{9,10},{10,1... | collective-permute-start | bytes 1671176 | tf_op jit(solution)/shard_map/ppermute | solution.py:307
  46.0 0.0 collective-permute-done.5.refs_4_
  46.0 5.1 %collective-permute-start.6 = (bf16[272,1024]{1,0:T(8,128)(2,1)S(1)}, bf16[272,1024]{1,0:T(8,128)(2,1)}, u32[]{:S(2)}, u32[]{:S(2)}) collective-permute-start(bf16[272,1024]{1,0:T(8,128)(2,1)S(1)} %collective-permute-done.5.refs_4_), channel_id=1, source_target_pairs={{0,7},{1,0},{2,1},{3,2},{4,3},{5,4},{6,5},{7,6},{8,15},{9,8},{10,9... | collective-permute-start | bytes 1671176 | tf_op jit(solution)/shard_map/ppermute | solution.py:308
  51.1 0.0 copy-start.2
  51.1 0.8 copy-done.2
  52.0 8.3 %collective-permute-done.2.refs_5_ = bf16[272,1024]{1,0:T(8,128)(2,1)} collective-permute-done((bf16[272,1024]{1,0:T(8,128)(2,1)S(1)}, bf16[272,1024]{1,0:T(8,128)(2,1)}, u32[]{:S(2)}, u32[]{:S(2)}) %collective-permute-start.2) | collective-permute-done | bytes 557088 | tf_op jit(solution)/shard_map/ppermute | solution.py:307
  60.3 1.9 %collective-permute-start.3 = (bf16[272,1024]{1,0:T(8,128)(2,1)}, bf16[272,1024]{1,0:T(8,128)(2,1)S(1)}, u32[]{:S(2)}, u32[]{:S(2)}) collective-permute-start(bf16[272,1024]{1,0:T(8,128)(2,1)} %collective-permute-done.2.refs_5_), channel_id=1, source_target_pairs={{0,1},{1,2},{2,3},{3,4},{4,5},{5,6},{6,7},{7,0},{8,9},{9,10},{10,1... | collective-permute-start | bytes 1671176 | tf_op jit(solution)/shard_map/ppermute | solution.py:307
  62.2 0.0 collective-permute-done.6.refs_6_
  62.2 0.0 copy-start.1
  62.2 1.0 copy-done.1
  63.3 1.1 copy-done.3
  64.3 3.8 %shard_map.39 = (bf16[16,256,1024]{2,1,0:T(8,128)(2,1)S(1)}, bf16[16,256,128]{2,1,0:T(8,128)(2,1)S(1)}) custom-call(s32[1]{0:T(128)} %bitcast.place_ref, bf16[272,1024]{1,0:T(8,128)(2,1)S(1)} %copy-done.1, bf16[272,1024]{1,0:T(8,128)(2,1)S(1)} %collective-permute-done.refs_1_, bf16[272,1024]{1,0:T(8,128)(2,1)S(1)} %collective-permute-done.4.refs_2_, ...), custom_call_target="tpu_custom_call" | custom-call | tf_op jit(solution)/shard_map/pallas_call | solution.py:149
  68.2 0.0 copy-start
  68.2 3.2 %copy-done = bf16[16,256,1024]{2,1,0:T(8,128)(2,1)} copy-done((bf16[16,256,1024]{2,1,0:T(8,128)(2,1)}, bf16[16,256,1024]{2,1,0:T(8,128)(2,1)S(1)}, u32[]{:S(2)}) %copy-start) | copy-done | bytes 8388632
  71.4 4.2 %collective-permute-done.3.last_ref = bf16[272,1024]{1,0:T(8,128)(2,1)S(1)} collective-permute-done((bf16[272,1024]{1,0:T(8,128)(2,1)}, bf16[272,1024]{1,0:T(8,128)(2,1)S(1)}, u32[]{:S(2)}, u32[]{:S(2)}) %collective-permute-start.3) | collective-permute-done | bytes 557088 | tf_op jit(solution)/shard_map/ppermute | solution.py:307
  75.6 0.3 all-gather.2.cloned.1.call-done.cols_hbm
  76.0 12.9 %shard_map.40 = f32[16,1,256]{2,1,0:T(1,128)S(1)} custom-call(s32[1]{0:T(128)} %bitcast.place_ref, bf16[272,1024]{1,0:T(8,128)(2,1)S(1)} %collective-permute-done.3.last_ref, bf16[16,256,1024]{2,1,0:T(8,128)(2,1)} %copy-done, bf16[16,256,128]{2,1,0:T(8,128)(2,1)S(1)} %get-tuple-element.11.slot_meta_hbm, bf16[4352,1024]{1,0:T(8,128)(2,1)} %all-gather.2.cloned.1.call-done.cols_hbm), custom_call_target="tpu_custom_call" | custom-call | tf_op jit(solution)/shard_map/pallas_call | solution.py:257
  88.9 0.1 reshape.20
  89.0 0.1 reshape.21
  89.1 14.4 %all_to_all.5.found_ref = f32[8,1,512]{2,1,0:T(1,128)} all-to-all(f32[8,1,512]{2,1,0:T(1,128)S(1)} %reshape.21), channel_id=1, replica_groups=mesh['x'=4,'z'=8,'core'=2,'y'=8] {'y'}, dimensions={0} | all-to-all | bytes 32768 | tf_op jit(solution)/shard_map/all_to_all | solution.py:320
  103.5 1.4 %shard_map.41 = f32[1,256]{1,0:T(1,128)} custom-call(f32[8,1,512]{2,1,0:T(1,128)} %all_to_all.5.found_ref, f32[2,256]{1,0:T(2,128)} %shard_map.38.own_ref), custom_call_target="tpu_custom_call" | custom-call | tf_op jit(solution)/shard_map/pallas_call | solution.py:290
  (3 shorter events, 0.1 us)
Async XLA Ops:
  6.5 69.4 %all-gather.2.cloned.1.call-start = ((), (), s32[]{:S(2)}) async-start(), calls=%async_computation.1 | async-start | bytes 9469952 | tf_op jit(solution)/shard_map/all_gather | solution.py:305
  9.0 18.2 %collective-permute-start = (bf16[272,1024]{1,0:T(8,128)(2,1)}, bf16[272,1024]{1,0:T(8,128)(2,1)S(1)}, u32[]{:S(2)}, u32[]{:S(2)}) collective-permute-start(bf16[272,1024]{1,0:T(8,128)(2,1)} %shard_map.37.refs_0_), channel_id=1, source_target_pairs={{0,1},{1,2},{2,3},{3,4},{4,5},{5,6},{6,7},{7,0},{8,9},{9,10},{10,1... | collective-permute-start | bytes 1671176 | tf_op jit(solution)/shard_map/ppermute | solution.py:307
  12.4 16.6 %collective-permute-start.4 = (bf16[272,1024]{1,0:T(8,128)(2,1)}, bf16[272,1024]{1,0:T(8,128)(2,1)S(1)}, u32[]{:S(2)}, u32[]{:S(2)}) collective-permute-start(bf16[272,1024]{1,0:T(8,128)(2,1)} %shard_map.37.refs_0_), channel_id=1, source_target_pairs={{0,7},{1,0},{2,1},{3,2},{4,3},{5,4},{6,5},{7,6},{8,15},{9,8},{10,9... | collective-permute-start | bytes 1671176 | tf_op jit(solution)/shard_map/ppermute | solution.py:308
  27.2 16.9 %collective-permute-start.1 = (bf16[272,1024]{1,0:T(8,128)(2,1)S(1)}, bf16[272,1024]{1,0:T(8,128)(2,1)S(1)}, u32[]{:S(2)}, u32[]{:S(2)}) collective-permute-start(bf16[272,1024]{1,0:T(8,128)(2,1)S(1)} %collective-permute-done.refs_1_), channel_id=1, source_target_pairs={{0,1},{1,2},{2,3},{3,4},{4,5},{5,6},{6,7},{7,0},{8,9},{9,10},{10,1... | collective-permute-start | bytes 1671176 | tf_op jit(solution)/shard_map/ppermute | solution.py:307
  29.1 16.9 %collective-permute-start.5 = (bf16[272,1024]{1,0:T(8,128)(2,1)S(1)}, bf16[272,1024]{1,0:T(8,128)(2,1)S(1)}, u32[]{:S(2)}, u32[]{:S(2)}) collective-permute-start(bf16[272,1024]{1,0:T(8,128)(2,1)S(1)} %collective-permute-done.4.refs_2_), channel_id=1, source_target_pairs={{0,7},{1,0},{2,1},{3,2},{4,3},{5,4},{6,5},{7,6},{8,15},{9,8},{10,9... | collective-permute-start | bytes 1671176 | tf_op jit(solution)/shard_map/ppermute | solution.py:308
  44.1 16.2 %collective-permute-start.2 = (bf16[272,1024]{1,0:T(8,128)(2,1)S(1)}, bf16[272,1024]{1,0:T(8,128)(2,1)}, u32[]{:S(2)}, u32[]{:S(2)}) collective-permute-start(bf16[272,1024]{1,0:T(8,128)(2,1)S(1)} %collective-permute-done.1.refs_3_), channel_id=1, source_target_pairs={{0,1},{1,2},{2,3},{3,4},{4,5},{5,6},{6,7},{7,0},{8,9},{9,10},{10,1... | collective-permute-start | bytes 1671176 | tf_op jit(solution)/shard_map/ppermute | solution.py:307
  46.0 16.2 %collective-permute-start.6 = (bf16[272,1024]{1,0:T(8,128)(2,1)S(1)}, bf16[272,1024]{1,0:T(8,128)(2,1)}, u32[]{:S(2)}, u32[]{:S(2)}) collective-permute-start(bf16[272,1024]{1,0:T(8,128)(2,1)S(1)} %collective-permute-done.5.refs_4_), channel_id=1, source_target_pairs={{0,7},{1,0},{2,1},{3,2},{4,3},{5,4},{6,5},{7,6},{8,15},{9,8},{10,9... | collective-permute-start | bytes 1671176 | tf_op jit(solution)/shard_map/ppermute | solution.py:308
  51.1 0.8 copy-start.2
  60.3 15.4 %collective-permute-start.3 = (bf16[272,1024]{1,0:T(8,128)(2,1)}, bf16[272,1024]{1,0:T(8,128)(2,1)S(1)}, u32[]{:S(2)}, u32[]{:S(2)}) collective-permute-start(bf16[272,1024]{1,0:T(8,128)(2,1)} %collective-permute-done.2.refs_5_), channel_id=1, source_target_pairs={{0,1},{1,2},{2,3},{3,4},{4,5},{5,6},{6,7},{7,0},{8,9},{9,10},{10,1... | collective-permute-start | bytes 1671176 | tf_op jit(solution)/shard_map/ppermute | solution.py:307
  62.2 1.1 copy-start.1
  63.3 1.1 copy-start.3
  68.2 3.3 %copy-start = (bf16[16,256,1024]{2,1,0:T(8,128)(2,1)}, bf16[16,256,1024]{2,1,0:T(8,128)(2,1)S(1)}, u32[]{:S(2)}) copy-start(bf16[16,256,1024]{2,1,0:T(8,128)(2,1)S(1)} %get-tuple-element.10.slots_hbm) | copy-start | bytes 25165828
Sparse Core Ops, SparseCore 0:
  9.5 66.4 all-gather.1

commit v5 on v4

--- a/solution.py
+++ b/solution.py
@@ -187,10 +187,10 @@
     waited[0] = 0
     last_slots[...], last_meta[...] = into_slots(last_ref[0:ROWS, :], last_ref[ROWS:AUG, 0:ROWS])
     weights = spread_weights()
+    for copy in [*tops, team(0), *rests]:
+        copy.start()
     for copy in notes:
         copy.wait()
-    for copy in [*tops, team(0)]:
-        copy.start()
     for b in range(blocks):
         meta = tall(held[b, ROWS:AUG, 0:ROWS])
         held_lanes[b] = jnp.dot(meta, weights, preferred_element_type=jnp.float32)
@@ -206,8 +206,6 @@
     table.wait()
     for copy in tops:
         copy.wait()
-    for copy in rests:
-        copy.start()
     groups = blocks * WINDOW // 8
 
     def cluster(g):

time: 112 us -> 112 us (level)
  no operation moved by 1% of the time
where the time goes in v5:
time: 112 us; the launch traced here: 111 us
  waiting for transfers between devices  31.7 us (28%)
  starting transfers between devices  23.3 us (21%)
  Pallas kernels  21.8 us (19%)
  blocking collectives  14.4 us (13%)
  between operations  13.6 us (12%)
  local copies, waits for them, and re-layouts  6.36 us (6%)
    ppermute x4, waiting for transfers between devices, per_device(): up = lambda v: lax.ppermute(v, 'y', ring(8, 1))  31.3 us
    all_to_all x1, blocking collectives, per_device(): lax.all_to_all(found, 'y', split_axis=0, concat_axis=0, tiled=True)  14.4 us
    ppermute x3, starting transfers between devices, per_device(): down = lambda v: lax.ppermute(v, 'y', ring(8, -1))  14.1 us
    pallas_call x1, Pallas kernels, match(): pl.pallas_call(functools.partial(match_kernel, offset), out_shape=jax.Sha...  12.2 us
    ppermute x4, starting transfers between devices, per_device(): up = lambda v: lax.ppermute(v, 'y', ring(8, 1))  9.21 us
    unnamed x8, local copies, waits for them, and re-layouts  6.17 us
    pallas_call x2, Pallas kernels, own_call(): pl.pallas_call(kernel, out_shape=out, in_specs=[pl.BlockSpec(memory_space...  4.32 us
    pallas_call x1, Pallas kernels, spread(): pl.pallas_call(functools.partial(spread_kernel, offsets), out_shape=(jax....  3.84 us
  transfers between devices with their start and end apart: 8, of which 5 were waited for; matrix products, arithmetic and copies ran while one was open for 0% of the time, Pallas kernels for 5%

profile of v5, /device:TPU:2, one launch (start us, length us, event | category | flops | bytes accessed | tf_op | source)
XLA Modules:
  0.0 111.1 jit_solution(6647906701139455548)
XLA Ops:
  6.5 0.0 all-gather.2.cloned.1.call-start
  6.5 2.4 %shard_map.37.refs_0_ = bf16[272,1024]{1,0:T(8,128)(2,1)} custom-call(bf16[256,1024]{1,0:T(8,128)(2,1)} %x_hbm.3, s32[1,256]{1,0:T(1,128)} %bitcast.8, s32[1,256]{1,0:T(1,128)} %bitcast.10), custom_call_target="tpu_custom_call" | custom-call | tf_op jit(solution)/shard_map/pallas_call | solution.py:93
  8.9 0.0 all-gather.2.cloned.1.call-update
  9.0 3.5 %collective-permute-start = (bf16[272,1024]{1,0:T(8,128)(2,1)}, bf16[272,1024]{1,0:T(8,128)(2,1)S(1)}, u32[]{:S(2)}, u32[]{:S(2)}) collective-permute-start(bf16[272,1024]{1,0:T(8,128)(2,1)} %shard_map.37.refs_0_), channel_id=1, source_target_pairs={{0,1},{1,2},{2,3},{3,4},{4,5},{5,6},{6,7},{7,0},{8,9},{9,10},{10,1... | collective-permute-start | bytes 1671176 | tf_op jit(solution)/shard_map/ppermute | solution.py:305
  12.4 3.8 %collective-permute-start.4 = (bf16[272,1024]{1,0:T(8,128)(2,1)}, bf16[272,1024]{1,0:T(8,128)(2,1)S(1)}, u32[]{:S(2)}, u32[]{:S(2)}) collective-permute-start(bf16[272,1024]{1,0:T(8,128)(2,1)} %shard_map.37.refs_0_), channel_id=1, source_target_pairs={{0,7},{1,0},{2,1},{3,2},{4,3},{5,4},{6,5},{7,6},{8,15},{9,8},{10,9... | collective-permute-start | bytes 1671176 | tf_op jit(solution)/shard_map/ppermute | solution.py:306
  16.3 1.9 %shard_map.38.own_ref = f32[2,256]{1,0:T(2,128)} custom-call(bf16[256,1024]{1,0:T(8,128)(2,1)} %x_hbm.3, s32[1,256]{1,0:T(1,128)} %bitcast.9, s32[1,256]{1,0:T(1,128)} %bitcast.11), custom_call_target="tpu_custom_call" | custom-call | tf_op jit(solution)/shard_map/pallas_call | solution.py:93
  18.2 8.9 %collective-permute-done.refs_1_ = bf16[272,1024]{1,0:T(8,128)(2,1)S(1)} collective-permute-done((bf16[272,1024]{1,0:T(8,128)(2,1)}, bf16[272,1024]{1,0:T(8,128)(2,1)S(1)}, u32[]{:S(2)}, u32[]{:S(2)}) %collective-permute-start) | collective-permute-done | bytes 557088 | tf_op jit(solution)/shard_map/ppermute | solution.py:305
  27.2 1.9 %collective-permute-start.1 = (bf16[272,1024]{1,0:T(8,128)(2,1)S(1)}, bf16[272,1024]{1,0:T(8,128)(2,1)S(1)}, u32[]{:S(2)}, u32[]{:S(2)}) collective-permute-start(bf16[272,1024]{1,0:T(8,128)(2,1)S(1)} %collective-permute-done.refs_1_), channel_id=1, source_target_pairs={{0,1},{1,2},{2,3},{3,4},{4,5},{5,6},{6,7},{7,0},{8,9},{9,10},{10,1... | collective-permute-start | bytes 1671176 | tf_op jit(solution)/shard_map/ppermute | solution.py:305
  29.1 0.0 collective-permute-done.4.refs_2_
  29.1 5.1 %collective-permute-start.5 = (bf16[272,1024]{1,0:T(8,128)(2,1)S(1)}, bf16[272,1024]{1,0:T(8,128)(2,1)S(1)}, u32[]{:S(2)}, u32[]{:S(2)}) collective-permute-start(bf16[272,1024]{1,0:T(8,128)(2,1)S(1)} %collective-permute-done.4.refs_2_), channel_id=1, source_target_pairs={{0,7},{1,0},{2,1},{3,2},{4,3},{5,4},{6,5},{7,6},{8,15},{9,8},{10,9... | collective-permute-start | bytes 1671176 | tf_op jit(solution)/shard_map/ppermute | solution.py:306
  34.2 9.8 %collective-permute-done.1.refs_3_ = bf16[272,1024]{1,0:T(8,128)(2,1)S(1)} collective-permute-done((bf16[272,1024]{1,0:T(8,128)(2,1)S(1)}, bf16[272,1024]{1,0:T(8,128)(2,1)S(1)}, u32[]{:S(2)}, u32[]{:S(2)}) %collective-permute-start.1) | collective-permute-done | bytes 557088 | tf_op jit(solution)/shard_map/ppermute | solution.py:305
  44.1 1.9 %collective-permute-start.2 = (bf16[272,1024]{1,0:T(8,128)(2,1)S(1)}, bf16[272,1024]{1,0:T(8,128)(2,1)}, u32[]{:S(2)}, u32[]{:S(2)}) collective-permute-start(bf16[272,1024]{1,0:T(8,128)(2,1)S(1)} %collective-permute-done.1.refs_3_), channel_id=1, source_target_pairs={{0,1},{1,2},{2,3},{3,4},{4,5},{5,6},{6,7},{7,0},{8,9},{9,10},{10,1... | collective-permute-start | bytes 1671176 | tf_op jit(solution)/shard_map/ppermute | solution.py:305
  46.0 0.0 collective-permute-done.5.refs_4_
  46.0 5.1 %collective-permute-start.6 = (bf16[272,1024]{1,0:T(8,128)(2,1)S(1)}, bf16[272,1024]{1,0:T(8,128)(2,1)}, u32[]{:S(2)}, u32[]{:S(2)}) collective-permute-start(bf16[272,1024]{1,0:T(8,128)(2,1)S(1)} %collective-permute-done.5.refs_4_), channel_id=1, source_target_pairs={{0,7},{1,0},{2,1},{3,2},{4,3},{5,4},{6,5},{7,6},{8,15},{9,8},{10,9... | collective-permute-start | bytes 1671176 | tf_op jit(solution)/shard_map/ppermute | solution.py:306
  51.1 0.0 copy-start.2
  51.1 0.8 copy-done.2
  52.0 8.3 %collective-permute-done.2.refs_5_ = bf16[272,1024]{1,0:T(8,128)(2,1)} collective-permute-done((bf16[272,1024]{1,0:T(8,128)(2,1)S(1)}, bf16[272,1024]{1,0:T(8,128)(2,1)}, u32[]{:S(2)}, u32[]{:S(2)}) %collective-permute-start.2) | collective-permute-done | bytes 557088 | tf_op jit(solution)/shard_map/ppermute | solution.py:305
  60.3 1.9 %collective-permute-start.3 = (bf16[272,1024]{1,0:T(8,128)(2,1)}, bf16[272,1024]{1,0:T(8,128)(2,1)S(1)}, u32[]{:S(2)}, u32[]{:S(2)}) collective-permute-start(bf16[272,1024]{1,0:T(8,128)(2,1)} %collective-permute-done.2.refs_5_), channel_id=1, source_target_pairs={{0,1},{1,2},{2,3},{3,4},{4,5},{5,6},{6,7},{7,0},{8,9},{9,10},{10,1... | collective-permute-start | bytes 1671176 | tf_op jit(solution)/shard_map/ppermute | solution.py:305
  62.2 0.0 collective-permute-done.6.refs_6_
  62.2 0.0 copy-start.1
  62.2 1.0 copy-done.1
  63.3 1.1 copy-done.3
  64.3 3.8 %shard_map.39 = (bf16[16,256,1024]{2,1,0:T(8,128)(2,1)S(1)}, bf16[16,256,128]{2,1,0:T(8,128)(2,1)S(1)}) custom-call(s32[1]{0:T(128)} %bitcast.place_ref, bf16[272,1024]{1,0:T(8,128)(2,1)S(1)} %copy-done.1, bf16[272,1024]{1,0:T(8,128)(2,1)S(1)} %collective-permute-done.refs_1_, bf16[272,1024]{1,0:T(8,128)(2,1)S(1)} %collective-permute-done.4.refs_2_, ...), custom_call_target="tpu_custom_call" | custom-call | tf_op jit(solution)/shard_map/pallas_call | solution.py:149
  68.2 0.0 copy-start
  68.2 3.2 %copy-done = bf16[16,256,1024]{2,1,0:T(8,128)(2,1)} copy-done((bf16[16,256,1024]{2,1,0:T(8,128)(2,1)}, bf16[16,256,1024]{2,1,0:T(8,128)(2,1)S(1)}, u32[]{:S(2)}) %copy-start) | copy-done | bytes 8388632
  71.4 4.2 %collective-permute-done.3.last_ref = bf16[272,1024]{1,0:T(8,128)(2,1)S(1)} collective-permute-done((bf16[272,1024]{1,0:T(8,128)(2,1)}, bf16[272,1024]{1,0:T(8,128)(2,1)S(1)}, u32[]{:S(2)}, u32[]{:S(2)}) %collective-permute-start.3) | collective-permute-done | bytes 557088 | tf_op jit(solution)/shard_map/ppermute | solution.py:305
  75.6 0.3 all-gather.2.cloned.1.call-done.cols_hbm
  76.0 12.2 %shard_map.40 = f32[16,1,256]{2,1,0:T(1,128)S(1)} custom-call(s32[1]{0:T(128)} %bitcast.place_ref, bf16[272,1024]{1,0:T(8,128)(2,1)S(1)} %collective-permute-done.3.last_ref, bf16[16,256,1024]{2,1,0:T(8,128)(2,1)} %copy-done, bf16[16,256,128]{2,1,0:T(8,128)(2,1)S(1)} %get-tuple-element.11.slot_meta_hbm, bf16[4352,1024]{1,0:T(8,128)(2,1)} %all-gather.2.cloned.1.call-done.cols_hbm), custom_call_target="tpu_custom_call" | custom-call | tf_op jit(solution)/shard_map/pallas_call | solution.py:255
  88.2 0.1 reshape.20
  88.3 0.1 reshape.21
  88.4 14.4 %all_to_all.5.found_ref = f32[8,1,512]{2,1,0:T(1,128)} all-to-all(f32[8,1,512]{2,1,0:T(1,128)S(1)} %reshape.21), channel_id=1, replica_groups=mesh['x'=4,'z'=8,'core'=2,'y'=8] {'y'}, dimensions={0} | all-to-all | bytes 32768 | tf_op jit(solution)/shard_map/all_to_all | solution.py:318
  102.8 1.4 %shard_map.41 = f32[1,256]{1,0:T(1,128)} custom-call(f32[8,1,512]{2,1,0:T(1,128)} %all_to_all.5.found_ref, f32[2,256]{1,0:T(2,128)} %shard_map.38.own_ref), custom_call_target="tpu_custom_call" | custom-call | tf_op jit(solution)/shard_map/pallas_call | solution.py:288
  (3 shorter events, 0.1 us)
Async XLA Ops:
  6.5 69.4 %all-gather.2.cloned.1.call-start = ((), (), s32[]{:S(2)}) async-start(), calls=%async_computation.1 | async-start | bytes 9469952 | tf_op jit(solution)/shard_map/all_gather | solution.py:303
  9.0 18.2 %collective-permute-start = (bf16[272,1024]{1,0:T(8,128)(2,1)}, bf16[272,1024]{1,0:T(8,128)(2,1)S(1)}, u32[]{:S(2)}, u32[]{:S(2)}) collective-permute-start(bf16[272,1024]{1,0:T(8,128)(2,1)} %shard_map.37.refs_0_), channel_id=1, source_target_pairs={{0,1},{1,2},{2,3},{3,4},{4,5},{5,6},{6,7},{7,0},{8,9},{9,10},{10,1... | collective-permute-start | bytes 1671176 | tf_op jit(solution)/shard_map/ppermute | solution.py:305
  12.4 16.6 %collective-permute-start.4 = (bf16[272,1024]{1,0:T(8,128)(2,1)}, bf16[272,1024]{1,0:T(8,128)(2,1)S(1)}, u32[]{:S(2)}, u32[]{:S(2)}) collective-permute-start(bf16[272,1024]{1,0:T(8,128)(2,1)} %shard_map.37.refs_0_), channel_id=1, source_target_pairs={{0,7},{1,0},{2,1},{3,2},{4,3},{5,4},{6,5},{7,6},{8,15},{9,8},{10,9... | collective-permute-start | bytes 1671176 | tf_op jit(solution)/shard_map/ppermute | solution.py:306
  27.2 16.9 %collective-permute-start.1 = (bf16[272,1024]{1,0:T(8,128)(2,1)S(1)}, bf16[272,1024]{1,0:T(8,128)(2,1)S(1)}, u32[]{:S(2)}, u32[]{:S(2)}) collective-permute-start(bf16[272,1024]{1,0:T(8,128)(2,1)S(1)} %collective-permute-done.refs_1_), channel_id=1, source_target_pairs={{0,1},{1,2},{2,3},{3,4},{4,5},{5,6},{6,7},{7,0},{8,9},{9,10},{10,1... | collective-permute-start | bytes 1671176 | tf_op jit(solution)/shard_map/ppermute | solution.py:305
  29.1 16.9 %collective-permute-start.5 = (bf16[272,1024]{1,0:T(8,128)(2,1)S(1)}, bf16[272,1024]{1,0:T(8,128)(2,1)S(1)}, u32[]{:S(2)}, u32[]{:S(2)}) collective-permute-start(bf16[272,1024]{1,0:T(8,128)(2,1)S(1)} %collective-permute-done.4.refs_2_), channel_id=1, source_target_pairs={{0,7},{1,0},{2,1},{3,2},{4,3},{5,4},{6,5},{7,6},{8,15},{9,8},{10,9... | collective-permute-start | bytes 1671176 | tf_op jit(solution)/shard_map/ppermute | solution.py:306
  44.1 16.2 %collective-permute-start.2 = (bf16[272,1024]{1,0:T(8,128)(2,1)S(1)}, bf16[272,1024]{1,0:T(8,128)(2,1)}, u32[]{:S(2)}, u32[]{:S(2)}) collective-permute-start(bf16[272,1024]{1,0:T(8,128)(2,1)S(1)} %collective-permute-done.1.refs_3_), channel_id=1, source_target_pairs={{0,1},{1,2},{2,3},{3,4},{4,5},{5,6},{6,7},{7,0},{8,9},{9,10},{10,1... | collective-permute-start | bytes 1671176 | tf_op jit(solution)/shard_map/ppermute | solution.py:305
  46.0 16.2 %collective-permute-start.6 = (bf16[272,1024]{1,0:T(8,128)(2,1)S(1)}, bf16[272,1024]{1,0:T(8,128)(2,1)}, u32[]{:S(2)}, u32[]{:S(2)}) collective-permute-start(bf16[272,1024]{1,0:T(8,128)(2,1)S(1)} %collective-permute-done.5.refs_4_), channel_id=1, source_target_pairs={{0,7},{1,0},{2,1},{3,2},{4,3},{5,4},{6,5},{7,6},{8,15},{9,8},{10,9... | collective-permute-start | bytes 1671176 | tf_op jit(solution)/shard_map/ppermute | solution.py:306
  51.1 0.8 copy-start.2
  60.3 15.4 %collective-permute-start.3 = (bf16[272,1024]{1,0:T(8,128)(2,1)}, bf16[272,1024]{1,0:T(8,128)(2,1)S(1)}, u32[]{:S(2)}, u32[]{:S(2)}) collective-permute-start(bf16[272,1024]{1,0:T(8,128)(2,1)} %collective-permute-done.2.refs_5_), channel_id=1, source_target_pairs={{0,1},{1,2},{2,3},{3,4},{4,5},{5,6},{6,7},{7,0},{8,9},{9,10},{10,1... | collective-permute-start | bytes 1671176 | tf_op jit(solution)/shard_map/ppermute | solution.py:305
  62.2 1.1 copy-start.1
  63.3 1.1 copy-start.3
  68.2 3.3 %copy-start = (bf16[16,256,1024]{2,1,0:T(8,128)(2,1)}, bf16[16,256,1024]{2,1,0:T(8,128)(2,1)S(1)}, u32[]{:S(2)}) copy-start(bf16[16,256,1024]{2,1,0:T(8,128)(2,1)S(1)} %get-tuple-element.10.slots_hbm) | copy-start | bytes 25165828
Sparse Core Ops, SparseCore 0:
  9.5 66.4 all-gather.1

commit v6 on v5

--- a/solution.py
+++ b/solution.py
@@ -165,8 +165,8 @@
 
 
 def match_kernel(
-    offset, place_ref, last_ref, slots_hbm, slot_meta_hbm, cols_hbm, out_ref,
-    held, held_lanes, slots, slot_meta, slot_lines, last_slots, last_meta, starts_vmem, table_ref, waited, sem,
+    offset, place_ref, last_hbm, slots_hbm, slot_meta_hbm, cols_hbm, out_ref,
+    held, held_lanes, slots, slot_meta, slot_lines, last_ref, last_slots, last_meta, starts_vmem, table_ref, waited, sem,
 ):
     blocks = cols_hbm.shape[0] // AUG
 
@@ -182,9 +182,11 @@
     tops = [part(b, 0, TOP, 1) for b in range(blocks)]
     rests = [part(b, TOP, ROWS, 2) for b in range(blocks)]
     small = pltpu.make_async_copy(slot_meta_hbm, slot_meta, sem.at[4, 0])
-    for copy in [*notes, small]:
+    last = pltpu.make_async_copy(last_hbm, last_ref, sem.at[4, 2])
+    for copy in [last, *notes, small]:
         copy.start()
     waited[0] = 0
+    last.wait()
     last_slots[...], last_meta[...] = into_slots(last_ref[0:ROWS, :], last_ref[ROWS:AUG, 0:ROWS])
     weights = spread_weights()
     for copy in [*tops, team(0), *rests]:
@@ -255,7 +257,7 @@
     return pl.pallas_call(
         functools.partial(match_kernel, offset),
         out_shape=jax.ShapeDtypeStruct((CLUSTERS, 1, 8 * SLOTS), jnp.float32),
-        in_specs=[smem, vmem, hbm, hbm, hbm],
+        in_specs=[smem, hbm, hbm, hbm, hbm],
         out_specs=vmem,
         scratch_shapes=[
             pltpu.VMEM((blocks, AUG, width), jnp.bfloat16),
@@ -263,6 +265,7 @@
             pltpu.VMEM((CLUSTERS, 8 * SLOTS, width), jnp.bfloat16),
             pltpu.VMEM((CLUSTERS, 8 * SLOTS, 128), jnp.bfloat16),
             pltpu.VMEM((CLUSTERS, 8, 8 * SLOTS), jnp.float32),
+            pltpu.VMEM((AUG, width), jnp.bfloat16),
             pltpu.VMEM((CLUSTERS, SLOTS, width), jnp.bfloat16),
             pltpu.VMEM((CLUSTERS, SLOTS, 128), jnp.bfloat16),
             pltpu.VMEM((blocks, 128), jnp.int32),

time: 112 us -> 112 us (level)
  no operation moved by 1% of the time
where the time goes in v6:
time: 112 us; the launch traced here: 111 us
  waiting for transfers between devices  31.7 us (28%)
  starting transfers between devices  23.3 us (21%)
  Pallas kernels  21.8 us (19%)
  blocking collectives  14.4 us (13%)
  between operations  13.6 us (12%)
  local copies, waits for them, and re-layouts  6.36 us (6%)
    ppermute x4, waiting for transfers between devices, per_device(): up = lambda v: lax.ppermute(v, 'y', ring(8, 1))  31.3 us
    all_to_all x1, blocking collectives, per_device(): lax.all_to_all(found, 'y', split_axis=0, concat_axis=0, tiled=True)  14.4 us
    ppermute x3, starting transfers between devices, per_device(): down = lambda v: lax.ppermute(v, 'y', ring(8, -1))  14.1 us
    pallas_call x1, Pallas kernels, match(): pl.pallas_call(functools.partial(match_kernel, offset), out_shape=jax.Sha...  12.2 us
    ppermute x4, starting transfers between devices, per_device(): up = lambda v: lax.ppermute(v, 'y', ring(8, 1))  9.21 us
    unnamed x8, local copies, waits for them, and re-layouts  6.17 us
    pallas_call x2, Pallas kernels, own_call(): pl.pallas_call(kernel, out_shape=out, in_specs=[pl.BlockSpec(memory_space...  4.32 us
    pallas_call x1, Pallas kernels, spread(): pl.pallas_call(functools.partial(spread_kernel, offsets), out_shape=(jax....  3.84 us
  transfers between devices with their start and end apart: 8, of which 5 were waited for; matrix products, arithmetic and copies ran while one was open for 0% of the time, Pallas kernels for 5%

profile of v6, /device:TPU:2, one launch (start us, length us, event | category | flops | bytes accessed | tf_op | source)
XLA Modules:
  0.0 111.1 jit_solution(13656444508219939713)
XLA Ops:
  6.5 0.0 all-gather.2.cloned.1.call-start
  6.5 2.4 %shard_map.37.refs_0_ = bf16[272,1024]{1,0:T(8,128)(2,1)} custom-call(bf16[256,1024]{1,0:T(8,128)(2,1)} %x_hbm.3, s32[1,256]{1,0:T(1,128)} %bitcast.8, s32[1,256]{1,0:T(1,128)} %bitcast.10), custom_call_target="tpu_custom_call" | custom-call | tf_op jit(solution)/shard_map/pallas_call | solution.py:93
  8.9 0.0 all-gather.2.cloned.1.call-update
  9.0 3.5 %collective-permute-start = (bf16[272,1024]{1,0:T(8,128)(2,1)}, bf16[272,1024]{1,0:T(8,128)(2,1)S(1)}, u32[]{:S(2)}, u32[]{:S(2)}) collective-permute-start(bf16[272,1024]{1,0:T(8,128)(2,1)} %shard_map.37.refs_0_), channel_id=1, source_target_pairs={{0,1},{1,2},{2,3},{3,4},{4,5},{5,6},{6,7},{7,0},{8,9},{9,10},{10,1... | collective-permute-start | bytes 1671176 | tf_op jit(solution)/shard_map/ppermute | solution.py:308
  12.4 3.8 %collective-permute-start.4 = (bf16[272,1024]{1,0:T(8,128)(2,1)}, bf16[272,1024]{1,0:T(8,128)(2,1)S(1)}, u32[]{:S(2)}, u32[]{:S(2)}) collective-permute-start(bf16[272,1024]{1,0:T(8,128)(2,1)} %shard_map.37.refs_0_), channel_id=1, source_target_pairs={{0,7},{1,0},{2,1},{3,2},{4,3},{5,4},{6,5},{7,6},{8,15},{9,8},{10,9... | collective-permute-start | bytes 1671176 | tf_op jit(solution)/shard_map/ppermute | solution.py:309
  16.3 1.9 %shard_map.38.own_ref = f32[2,256]{1,0:T(2,128)} custom-call(bf16[256,1024]{1,0:T(8,128)(2,1)} %x_hbm.3, s32[1,256]{1,0:T(1,128)} %bitcast.9, s32[1,256]{1,0:T(1,128)} %bitcast.11), custom_call_target="tpu_custom_call" | custom-call | tf_op jit(solution)/shard_map/pallas_call | solution.py:93
  18.2 8.9 %collective-permute-done.refs_1_ = bf16[272,1024]{1,0:T(8,128)(2,1)S(1)} collective-permute-done((bf16[272,1024]{1,0:T(8,128)(2,1)}, bf16[272,1024]{1,0:T(8,128)(2,1)S(1)}, u32[]{:S(2)}, u32[]{:S(2)}) %collective-permute-start) | collective-permute-done | bytes 557088 | tf_op jit(solution)/shard_map/ppermute | solution.py:308
  27.2 1.9 %collective-permute-start.1 = (bf16[272,1024]{1,0:T(8,128)(2,1)S(1)}, bf16[272,1024]{1,0:T(8,128)(2,1)S(1)}, u32[]{:S(2)}, u32[]{:S(2)}) collective-permute-start(bf16[272,1024]{1,0:T(8,128)(2,1)S(1)} %collective-permute-done.refs_1_), channel_id=1, source_target_pairs={{0,1},{1,2},{2,3},{3,4},{4,5},{5,6},{6,7},{7,0},{8,9},{9,10},{10,1... | collective-permute-start | bytes 1671176 | tf_op jit(solution)/shard_map/ppermute | solution.py:308
  29.1 0.0 collective-permute-done.4.refs_2_
  29.1 5.1 %collective-permute-start.5 = (bf16[272,1024]{1,0:T(8,128)(2,1)S(1)}, bf16[272,1024]{1,0:T(8,128)(2,1)S(1)}, u32[]{:S(2)}, u32[]{:S(2)}) collective-permute-start(bf16[272,1024]{1,0:T(8,128)(2,1)S(1)} %collective-permute-done.4.refs_2_), channel_id=1, source_target_pairs={{0,7},{1,0},{2,1},{3,2},{4,3},{5,4},{6,5},{7,6},{8,15},{9,8},{10,9... | collective-permute-start | bytes 1671176 | tf_op jit(solution)/shard_map/ppermute | solution.py:309
  34.2 9.8 %collective-permute-done.1.refs_3_ = bf16[272,1024]{1,0:T(8,128)(2,1)S(1)} collective-permute-done((bf16[272,1024]{1,0:T(8,128)(2,1)S(1)}, bf16[272,1024]{1,0:T(8,128)(2,1)S(1)}, u32[]{:S(2)}, u32[]{:S(2)}) %collective-permute-start.1) | collective-permute-done | bytes 557088 | tf_op jit(solution)/shard_map/ppermute | solution.py:308
  44.1 1.9 %collective-permute-start.2 = (bf16[272,1024]{1,0:T(8,128)(2,1)S(1)}, bf16[272,1024]{1,0:T(8,128)(2,1)}, u32[]{:S(2)}, u32[]{:S(2)}) collective-permute-start(bf16[272,1024]{1,0:T(8,128)(2,1)S(1)} %collective-permute-done.1.refs_3_), channel_id=1, source_target_pairs={{0,1},{1,2},{2,3},{3,4},{4,5},{5,6},{6,7},{7,0},{8,9},{9,10},{10,1... | collective-permute-start | bytes 1671176 | tf_op jit(solution)/shard_map/ppermute | solution.py:308
  46.0 0.0 collective-permute-done.5.refs_4_
  46.0 5.1 %collective-permute-start.6 = (bf16[272,1024]{1,0:T(8,128)(2,1)S(1)}, bf16[272,1024]{1,0:T(8,128)(2,1)}, u32[]{:S(2)}, u32[]{:S(2)}) collective-permute-start(bf16[272,1024]{1,0:T(8,128)(2,1)S(1)} %collective-permute-done.5.refs_4_), channel_id=1, source_target_pairs={{0,7},{1,0},{2,1},{3,2},{4,3},{5,4},{6,5},{7,6},{8,15},{9,8},{10,9... | collective-permute-start | bytes 1671176 | tf_op jit(solution)/shard_map/ppermute | solution.py:309
  51.1 0.0 copy-start.2
  51.1 0.8 copy-done.2
  52.0 8.3 %collective-permute-done.2.refs_5_ = bf16[272,1024]{1,0:T(8,128)(2,1)} collective-permute-done((bf16[272,1024]{1,0:T(8,128)(2,1)S(1)}, bf16[272,1024]{1,0:T(8,128)(2,1)}, u32[]{:S(2)}, u32[]{:S(2)}) %collective-permute-start.2) | collective-permute-done | bytes 557088 | tf_op jit(solution)/shard_map/ppermute | solution.py:308
  60.3 1.9 %collective-permute-start.3 = (bf16[272,1024]{1,0:T(8,128)(2,1)}, bf16[272,1024]{1,0:T(8,128)(2,1)S(1)}, u32[]{:S(2)}, u32[]{:S(2)}) collective-permute-start(bf16[272,1024]{1,0:T(8,128)(2,1)} %collective-permute-done.2.refs_5_), channel_id=1, source_target_pairs={{0,1},{1,2},{2,3},{3,4},{4,5},{5,6},{6,7},{7,0},{8,9},{9,10},{10,1... | collective-permute-start | bytes 1671176 | tf_op jit(solution)/shard_map/ppermute | solution.py:308
  62.2 0.0 collective-permute-done.6.refs_6_
  62.2 0.0 copy-start.1
  62.2 1.0 copy-done.1
  63.3 1.1 copy-done.3
  64.3 3.8 %shard_map.39 = (bf16[16,256,1024]{2,1,0:T(8,128)(2,1)S(1)}, bf16[16,256,128]{2,1,0:T(8,128)(2,1)S(1)}) custom-call(s32[1]{0:T(128)} %bitcast.place_ref, bf16[272,1024]{1,0:T(8,128)(2,1)S(1)} %copy-done.1, bf16[272,1024]{1,0:T(8,128)(2,1)S(1)} %collective-permute-done.refs_1_, bf16[272,1024]{1,0:T(8,128)(2,1)S(1)} %collective-permute-done.4.refs_2_, ...), custom_call_target="tpu_custom_call" | custom-call | tf_op jit(solution)/shard_map/pallas_call | solution.py:149
  68.2 0.0 copy-start
  68.2 3.2 %copy-done = bf16[16,256,1024]{2,1,0:T(8,128)(2,1)} copy-done((bf16[16,256,1024]{2,1,0:T(8,128)(2,1)}, bf16[16,256,1024]{2,1,0:T(8,128)(2,1)S(1)}, u32[]{:S(2)}) %copy-start) | copy-done | bytes 8388632
  71.4 4.2 %collective-permute-done.3.last_hbm = bf16[272,1024]{1,0:T(8,128)(2,1)S(1)} collective-permute-done((bf16[272,1024]{1,0:T(8,128)(2,1)}, bf16[272,1024]{1,0:T(8,128)(2,1)S(1)}, u32[]{:S(2)}, u32[]{:S(2)}) %collective-permute-start.3) | collective-permute-done | bytes 557088 | tf_op jit(solution)/shard_map/ppermute | solution.py:308
  75.6 0.3 all-gather.2.cloned.1.call-done.cols_hbm
  76.0 12.2 %shard_map.40 = f32[16,1,256]{2,1,0:T(1,128)S(1)} custom-call(s32[1]{0:T(128)} %bitcast.place_ref, bf16[272,1024]{1,0:T(8,128)(2,1)S(1)} %collective-permute-done.3.last_hbm, bf16[16,256,1024]{2,1,0:T(8,128)(2,1)} %copy-done, bf16[16,256,128]{2,1,0:T(8,128)(2,1)S(1)} %get-tuple-element.11.slot_meta_hbm, bf16[4352,1024]{1,0:T(8,128)(2,1)} %all-gather.2.cloned.1.call-done.cols_hbm), custom_call_target="tpu_custom_call" | custom-call | tf_op jit(solution)/shard_map/pallas_call | solution.py:257
  88.2 0.1 reshape.20
  88.3 0.1 reshape.21
  88.4 14.4 %all_to_all.5.found_ref = f32[8,1,512]{2,1,0:T(1,128)} all-to-all(f32[8,1,512]{2,1,0:T(1,128)S(1)} %reshape.21), channel_id=1, replica_groups=mesh['x'=4,'z'=8,'core'=2,'y'=8] {'y'}, dimensions={0} | all-to-all | bytes 32768 | tf_op jit(solution)/shard_map/all_to_all | solution.py:321
  102.8 1.4 %shard_map.41 = f32[1,256]{1,0:T(1,128)} custom-call(f32[8,1,512]{2,1,0:T(1,128)} %all_to_all.5.found_ref, f32[2,256]{1,0:T(2,128)} %shard_map.38.own_ref), custom_call_target="tpu_custom_call" | custom-call | tf_op jit(solution)/shard_map/pallas_call | solution.py:291
  (3 shorter events, 0.1 us)
Async XLA Ops:
  6.5 69.4 %all-gather.2.cloned.1.call-start = ((), (), s32[]{:S(2)}) async-start(), calls=%async_computation.1 | async-start | bytes 9469952 | tf_op jit(solution)/shard_map/all_gather | solution.py:306
  9.0 18.2 %collective-permute-start = (bf16[272,1024]{1,0:T(8,128)(2,1)}, bf16[272,1024]{1,0:T(8,128)(2,1)S(1)}, u32[]{:S(2)}, u32[]{:S(2)}) collective-permute-start(bf16[272,1024]{1,0:T(8,128)(2,1)} %shard_map.37.refs_0_), channel_id=1, source_target_pairs={{0,1},{1,2},{2,3},{3,4},{4,5},{5,6},{6,7},{7,0},{8,9},{9,10},{10,1... | collective-permute-start | bytes 1671176 | tf_op jit(solution)/shard_map/ppermute | solution.py:308
  12.4 16.6 %collective-permute-start.4 = (bf16[272,1024]{1,0:T(8,128)(2,1)}, bf16[272,1024]{1,0:T(8,128)(2,1)S(1)}, u32[]{:S(2)}, u32[]{:S(2)}) collective-permute-start(bf16[272,1024]{1,0:T(8,128)(2,1)} %shard_map.37.refs_0_), channel_id=1, source_target_pairs={{0,7},{1,0},{2,1},{3,2},{4,3},{5,4},{6,5},{7,6},{8,15},{9,8},{10,9... | collective-permute-start | bytes 1671176 | tf_op jit(solution)/shard_map/ppermute | solution.py:309
  27.2 16.9 %collective-permute-start.1 = (bf16[272,1024]{1,0:T(8,128)(2,1)S(1)}, bf16[272,1024]{1,0:T(8,128)(2,1)S(1)}, u32[]{:S(2)}, u32[]{:S(2)}) collective-permute-start(bf16[272,1024]{1,0:T(8,128)(2,1)S(1)} %collective-permute-done.refs_1_), channel_id=1, source_target_pairs={{0,1},{1,2},{2,3},{3,4},{4,5},{5,6},{6,7},{7,0},{8,9},{9,10},{10,1... | collective-permute-start | bytes 1671176 | tf_op jit(solution)/shard_map/ppermute | solution.py:308
  29.1 16.9 %collective-permute-start.5 = (bf16[272,1024]{1,0:T(8,128)(2,1)S(1)}, bf16[272,1024]{1,0:T(8,128)(2,1)S(1)}, u32[]{:S(2)}, u32[]{:S(2)}) collective-permute-start(bf16[272,1024]{1,0:T(8,128)(2,1)S(1)} %collective-permute-done.4.refs_2_), channel_id=1, source_target_pairs={{0,7},{1,0},{2,1},{3,2},{4,3},{5,4},{6,5},{7,6},{8,15},{9,8},{10,9... | collective-permute-start | bytes 1671176 | tf_op jit(solution)/shard_map/ppermute | solution.py:309
  44.1 16.2 %collective-permute-start.2 = (bf16[272,1024]{1,0:T(8,128)(2,1)S(1)}, bf16[272,1024]{1,0:T(8,128)(2,1)}, u32[]{:S(2)}, u32[]{:S(2)}) collective-permute-start(bf16[272,1024]{1,0:T(8,128)(2,1)S(1)} %collective-permute-done.1.refs_3_), channel_id=1, source_target_pairs={{0,1},{1,2},{2,3},{3,4},{4,5},{5,6},{6,7},{7,0},{8,9},{9,10},{10,1... | collective-permute-start | bytes 1671176 | tf_op jit(solution)/shard_map/ppermute | solution.py:308
  46.0 16.2 %collective-permute-start.6 = (bf16[272,1024]{1,0:T(8,128)(2,1)S(1)}, bf16[272,1024]{1,0:T(8,128)(2,1)}, u32[]{:S(2)}, u32[]{:S(2)}) collective-permute-start(bf16[272,1024]{1,0:T(8,128)(2,1)S(1)} %collective-permute-done.5.refs_4_), channel_id=1, source_target_pairs={{0,7},{1,0},{2,1},{3,2},{4,3},{5,4},{6,5},{7,6},{8,15},{9,8},{10,9... | collective-permute-start | bytes 1671176 | tf_op jit(solution)/shard_map/ppermute | solution.py:309
  51.1 0.8 copy-start.2
  60.3 15.4 %collective-permute-start.3 = (bf16[272,1024]{1,0:T(8,128)(2,1)}, bf16[272,1024]{1,0:T(8,128)(2,1)S(1)}, u32[]{:S(2)}, u32[]{:S(2)}) collective-permute-start(bf16[272,1024]{1,0:T(8,128)(2,1)} %collective-permute-done.2.refs_5_), channel_id=1, source_target_pairs={{0,1},{1,2},{2,3},{3,4},{4,5},{5,6},{6,7},{7,0},{8,9},{9,10},{10,1... | collective-permute-start | bytes 1671176 | tf_op jit(solution)/shard_map/ppermute | solution.py:308
  62.2 1.1 copy-start.1
  63.3 1.1 copy-start.3
  68.2 3.3 %copy-start = (bf16[16,256,1024]{2,1,0:T(8,128)(2,1)}, bf16[16,256,1024]{2,1,0:T(8,128)(2,1)S(1)}, u32[]{:S(2)}) copy-start(bf16[16,256,1024]{2,1,0:T(8,128)(2,1)S(1)} %get-tuple-element.10.slots_hbm) | copy-start | bytes 25165828
Sparse Core Ops, SparseCore 0:
  9.5 66.4 all-gather.1
